TPU v7x, 32 devices: a whole 2x2x4 slice. The times are simulated.
32 devices in a mesh: dp: 2 (over core), fsdp: 16 (over z, y, x).
Axes of the slice: x: 2, y: 2, z: 4, core: 2. Of those that a mesh axis runs over, the one named last changes fastest.
Arguments:
- x_regional: bfloat16 [1536, 512], P(('dp', 'fsdp')), may hold values from -6 to 6
- x_local: bfloat16 [1536, 49, 512], P(('dp', 'fsdp')), may hold values from -6 to 6
- w_qkv: bfloat16 [512, 1536], P('fsdp', 'dp'), may hold values from -0.25 to 0.25
- w_proj: bfloat16 [512, 512], P('fsdp', 'dp'), may hold values from -0.75 to 0.75
- w_fc1: bfloat16 [512, 2048], P('fsdp', 'dp'), may hold values from -0.25 to 0.25
- w_fc2: bfloat16 [2048, 512], P('fsdp', 'dp'), may hold values from -0.125 to 0.125
- gains: bfloat16 [3, 512], P(None, 'fsdp'), may hold values from 0.099609375 to 1.8984375
- biases: bfloat16 [11, 512], P(None, 'fsdp'), may hold values from -3 to 3
- region_counts: int32 [32], replicated, may hold values from 49 to 144, as said below
- cot_regional: bfloat16 [1536, 512], P(('dp', 'fsdp')), may hold values from -6 to 6
- cot_local: bfloat16 [1536, 49, 512], P(('dp', 'fsdp')), may hold values from -6 to 6
Outputs:
- out_regional: bfloat16 [1536, 512], P(('dp', 'fsdp'))
- out_local: bfloat16 [1536, 49, 512], P(('dp', 'fsdp'))
- grad_regional: bfloat16 [1536, 512], P(('dp', 'fsdp'))
- grad_local: bfloat16 [1536, 49, 512], P(('dp', 'fsdp'))
- grad_qkv: float32 [512, 1536], P('fsdp', 'dp')
- grad_proj: float32 [512, 512], P('fsdp', 'dp')
- grad_fc1: float32 [512, 2048], P('fsdp', 'dp')
- grad_fc2: float32 [2048, 512], P('fsdp', 'dp')
- grad_gains: float32 [3, 512], P(None, 'fsdp')
- grad_biases: float32 [11, 512], P(None, 'fsdp')
Inputs may be any that keep to these rules, and one draw needn't show every extreme that they name: `region_counts`: each count is 49, 81 or 144, and one of the first three is 144. Images occupy consecutive regions in order, starting at region 0; regions of an image that would pass region 1536 are cut off, and the images after it are empty.
All inputs are finite; a program needn't handle non-finite values.
Results may differ from a plain program's by a relative error of at most 0.02.
Values may be sent and summed in bfloat16 or wider, within the bound.
No kernel may reach another device: no remote copies, remote signals or barrier semaphores. Data moves between devices by JAX's collectives and lax.ppermute only.
A program may use at most 320 MiB of HBM per device.

v0:
```python
from functools import partial

import jax
import jax.numpy as jnp
from jax import lax
from jax.sharding import PartitionSpec as P

HEAD_DIM = 32
MAX_REGIONS = 144


EPSILON = 1e-05
NEGATIVE = -1e30


def shifted_2(x, axis, by):
    peers = lax.axis_size(axis)
    pairs = [(i, i + by) for i in range(peers) if 0 <= i + by < peers]
    return lax.ppermute(x, axis, pairs)


def norm_forward(values_in, norm_gain, norm_shift):
    centred = values_in - jnp.mean(values_in, axis=-1, keepdims=True)
    inv_std = lax.rsqrt(jnp.mean(centred * centred, axis=-1, keepdims=True) + EPSILON)
    normed = centred * inv_std
    return (normed * norm_gain + norm_shift, normed, inv_std)


def norm_backward(upstream, normed, inv_std, norm_gain):
    scaled = upstream * norm_gain
    centre_term = jnp.mean(scaled, axis=-1, keepdims=True)
    spread_term = jnp.mean(scaled * normed, axis=-1, keepdims=True)
    grad_values = inv_std * (scaled - centre_term - normed * spread_term)
    return (grad_values, jnp.sum(upstream * normed, axis=0), jnp.sum(upstream, axis=0))


def project_heads(normed, weight_full, bias_query, bias_value):
    model_width = weight_full.shape[0]
    rounded = normed.astype(jnp.bfloat16)
    projected = jnp.dot(rounded, weight_full, preferred_element_type=jnp.float32)
    queries = (projected[:, :model_width] + bias_query).astype(jnp.bfloat16)
    keys_in = projected[:, model_width : 2 * model_width].astype(jnp.bfloat16)
    values_in = (projected[:, 2 * model_width :] + bias_value).astype(jnp.bfloat16)
    return (rounded, queries, keys_in, values_in)


def score_block(queries, keys_in, allowed):
    scores = jnp.einsum(
        "bqhe,bkhe->bhqk", queries, keys_in, preferred_element_type=jnp.float32
    ) * HEAD_DIM ** (-0.5)
    if allowed is None:
        return scores
    return jnp.where(allowed[:, None], scores, NEGATIVE)


def attend_forward(queries, keys_in, values_in, allowed):
    scores = score_block(queries, keys_in, allowed)
    row_max = jnp.max(scores, axis=-1, keepdims=True)
    shifted = jnp.exp(scores - row_max)
    row_sum = jnp.sum(shifted, axis=-1, keepdims=True)
    weights = (shifted / row_sum).astype(jnp.bfloat16)
    attended = jnp.einsum("bhqk,bkhe->bqhe", weights, values_in, preferred_element_type=jnp.float32)
    return (attended.astype(jnp.bfloat16), row_max + jnp.log(row_sum))


def attend_backward(queries, keys_in, values_in, log_sums, upstream, allowed):
    scores = score_block(queries, keys_in, allowed)
    probability = jnp.exp(scores - log_sums)
    weights = probability.astype(jnp.bfloat16)
    grad_values = jnp.einsum(
        "bhqk,bqhe->bkhe", weights, upstream, preferred_element_type=jnp.float32
    )
    grad_probs = jnp.einsum(
        "bqhe,bkhe->bhqk", upstream, values_in, preferred_element_type=jnp.float32
    )
    grad_scores = probability * (
        grad_probs - jnp.sum(grad_probs * probability, axis=-1, keepdims=True)
    )
    grad_scores = grad_scores.astype(jnp.bfloat16)
    factor = HEAD_DIM ** (-0.5)
    grad_queries = (
        jnp.einsum("bhqk,bkhe->bqhe", grad_scores, keys_in, preferred_element_type=jnp.float32)
        * factor
    )
    grad_keys = (
        jnp.einsum("bhqk,bqhe->bkhe", grad_scores, queries, preferred_element_type=jnp.float32)
        * factor
    )
    return (grad_queries, grad_keys, grad_values)


def fetch_attention(w_qkv, w_proj, gains, biases):
    w_qkv, w_proj = (
        lax.all_gather(w_qkv, "dp", axis=1, tiled=True),
        lax.all_gather(w_proj, "dp", axis=1, tiled=True),
    )
    w_qkv, w_proj, gains, biases = (
        lax.all_gather(w_qkv, "fsdp", axis=0, tiled=True),
        lax.all_gather(w_proj, "fsdp", axis=0, tiled=True),
        lax.all_gather(gains, "fsdp", axis=1, tiled=True),
        lax.all_gather(biases, "fsdp", axis=1, tiled=True),
    )
    return (w_qkv, w_proj, gains.astype(jnp.float32), biases.astype(jnp.float32))


def fetch_mlp(w_fc1, w_fc2):
    w_fc1, w_fc2 = (
        lax.all_gather(w_fc1, "dp", axis=1, tiled=True),
        lax.all_gather(w_fc2, "dp", axis=1, tiled=True),
    )
    w_fc1, w_fc2 = (
        lax.all_gather(w_fc1, "fsdp", axis=0, tiled=True),
        lax.all_gather(w_fc2, "fsdp", axis=0, tiled=True),
    )
    return (w_fc1, w_fc2)


def on_device(
    x_regional,
    x_local,
    w_qkv,
    w_proj,
    w_fc1,
    w_fc2,
    gains,
    biases,
    region_counts,
    cot_regional,
    cot_local,
):
    regions_dev, local_len, model_width = x_local.shape
    window_len = local_len + 1
    head_count = model_width // HEAD_DIM
    span_dev = (regions_dev + MAX_REGIONS - 2) // regions_dev
    all_regions = regions_dev * lax.axis_size(("dp", "fsdp"))
    first_row = lax.axis_index(("dp", "fsdp")) * regions_dev
    qkv_full, proj_full, gain_full, bias_full = fetch_attention(w_qkv, w_proj, gains, biases)
    bias_rows = bias_full.shape[0]
    hidden_len = (bias_rows - 7) * model_width
    bias_query, bias_value, bias_proj = (bias_full[3], bias_full[4], bias_full[5])
    bias_up = bias_full[6 : bias_rows - 1].reshape(hidden_len)
    bias_down = bias_full[bias_rows - 1]
    region_in = x_regional.astype(jnp.float32)
    region_norm, region_hat, region_std = norm_forward(region_in, gain_full[0], bias_full[0])
    region_low, region_q, region_k, region_v = project_heads(
        region_norm, qkv_full, bias_query, bias_value
    )
    own_pair = jnp.concatenate([region_k, region_v], axis=1)
    near_list = []
    for offset in range(-span_dev, span_dev + 1):
        if offset == 0:
            near_list.append(own_pair)
        else:
            near_list.append(shifted_2(own_pair, ("dp", "fsdp"), -offset))
    near_pair = jnp.concatenate(near_list, axis=0)
    near_count = near_pair.shape[0]
    image_ends = jnp.minimum(jnp.cumsum(region_counts), all_regions)
    query_rows = first_row + jnp.arange(regions_dev, dtype=jnp.int32)
    key_rows = first_row - span_dev * regions_dev + jnp.arange(near_count, dtype=jnp.int32)
    query_image = jnp.sum((image_ends[None, :] <= query_rows[:, None]).astype(jnp.int32), axis=1)
    key_image = jnp.sum((image_ends[None, :] <= key_rows[:, None]).astype(jnp.int32), axis=1)
    inside = (key_rows >= 0) & (key_rows < all_regions)
    allowed = ((query_image[:, None] == key_image[None, :]) & inside[None, :])[None]
    heads_q = region_q.reshape(1, regions_dev, head_count, HEAD_DIM)
    heads_k = near_pair[:, :model_width].reshape(1, near_count, head_count, HEAD_DIM)
    heads_v = near_pair[:, model_width:].reshape(1, near_count, head_count, HEAD_DIM)
    region_att, region_lse = attend_forward(heads_q, heads_k, heads_v, allowed)
    region_att = region_att.reshape(regions_dev, model_width)
    region_mid = (
        region_in + jnp.dot(region_att, proj_full, preferred_element_type=jnp.float32) + bias_proj
    )
    flat_in = jnp.concatenate(
        [region_mid[:, None, :], x_local.astype(jnp.float32)], axis=1
    ).reshape(-1, model_width)
    norm_one, hat_one, std_one = norm_forward(flat_in, gain_full[1], bias_full[1])
    low_one, win_q, win_k, win_v = project_heads(norm_one, qkv_full, bias_query, bias_value)
    head_shape = (regions_dev, window_len, head_count, HEAD_DIM)
    win_q = win_q.reshape(head_shape)
    win_k = win_k.reshape(head_shape)
    win_v = win_v.reshape(head_shape)
    win_att, win_lse = attend_forward(win_q, win_k, win_v, None)
    win_att = win_att.reshape(-1, model_width)
    flat_mid = flat_in + jnp.dot(win_att, proj_full, preferred_element_type=jnp.float32) + bias_proj
    up_full, down_full = fetch_mlp(w_fc1, w_fc2)
    norm_two, hat_two, std_two = norm_forward(flat_mid, gain_full[2], bias_full[2])
    low_two = norm_two.astype(jnp.bfloat16)
    pre_act = jnp.dot(low_two, up_full, preferred_element_type=jnp.float32) + bias_up
    activated, gelu_back = jax.vjp(partial(jax.nn.gelu, approximate=False), pre_act)
    low_act = activated.astype(jnp.bfloat16)
    flat_out = (
        flat_mid + jnp.dot(low_act, down_full, preferred_element_type=jnp.float32) + bias_down
    )
    result = flat_out.reshape(regions_dev, window_len, model_width)
    out_regional = result[:, 0].astype(jnp.bfloat16)
    out_local = result[:, 1:].astype(jnp.bfloat16)
    up_full, down_full = fetch_mlp(w_fc1, w_fc2)
    upstream = jnp.concatenate(
        [cot_regional.astype(jnp.float32)[:, None, :], cot_local.astype(jnp.float32)], axis=1
    )
    upstream = upstream.reshape(-1, model_width)
    grad_out_low = upstream.astype(jnp.bfloat16)
    grad_down = jnp.einsum("nf,nd->fd", low_act, grad_out_low, preferred_element_type=jnp.float32)
    grad_bias_down = jnp.sum(grad_out_low.astype(jnp.float32), axis=0)
    grad_act = jnp.einsum("nd,fd->nf", grad_out_low, down_full, preferred_element_type=jnp.float32)
    grad_pre = gelu_back(grad_act)[0].astype(jnp.bfloat16)
    grad_up = jnp.einsum("nd,nf->df", low_two, grad_pre, preferred_element_type=jnp.float32)
    grad_bias_up = jnp.sum(grad_pre.astype(jnp.float32), axis=0)
    grad_norm_two = jnp.einsum("nf,df->nd", grad_pre, up_full, preferred_element_type=jnp.float32)
    grad_mid, grad_gain_two, grad_shift_two = norm_backward(
        grad_norm_two, hat_two, std_two, gain_full[2]
    )
    grad_mid = grad_mid + upstream
    qkv_full, proj_full, gain_full, bias_again = fetch_attention(w_qkv, w_proj, gains, biases)
    grad_proj_low = grad_mid.astype(jnp.bfloat16)
    grad_proj = jnp.einsum("nd,ne->de", win_att, grad_proj_low, preferred_element_type=jnp.float32)
    grad_bias_proj = jnp.sum(grad_proj_low.astype(jnp.float32), axis=0)
    grad_att = jnp.einsum("ne,de->nd", grad_proj_low, proj_full, preferred_element_type=jnp.float32)
    grad_att = grad_att.astype(jnp.bfloat16).reshape(head_shape)
    grad_wq, grad_wk, grad_wv = attend_backward(win_q, win_k, win_v, win_lse, grad_att, None)
    grad_mixed = jnp.concatenate(
        [
            grad_wq.reshape(-1, model_width),
            grad_wk.reshape(-1, model_width),
            grad_wv.reshape(-1, model_width),
        ],
        axis=1,
    ).astype(jnp.bfloat16)
    grad_qkv = jnp.einsum("nd,ne->de", low_one, grad_mixed, preferred_element_type=jnp.float32)
    grad_bias_q = jnp.sum(grad_mixed[:, :model_width].astype(jnp.float32), axis=0)
    grad_bias_v = jnp.sum(grad_mixed[:, 2 * model_width :].astype(jnp.float32), axis=0)
    grad_norm_one = jnp.einsum(
        "ne,de->nd", grad_mixed, qkv_full, preferred_element_type=jnp.float32
    )
    grad_in, grad_gain_one, grad_shift_one = norm_backward(
        grad_norm_one, hat_one, std_one, gain_full[1]
    )
    grad_in = (grad_in + grad_mid).reshape(regions_dev, window_len, model_width)
    grad_local = grad_in[:, 1:].astype(jnp.bfloat16)
    grad_region_mid = grad_in[:, 0]
    grad_rproj_low = grad_region_mid.astype(jnp.bfloat16)
    grad_proj = grad_proj + jnp.einsum(
        "nd,ne->de", region_att, grad_rproj_low, preferred_element_type=jnp.float32
    )
    grad_bias_proj = grad_bias_proj + jnp.sum(grad_rproj_low.astype(jnp.float32), axis=0)
    grad_ratt = jnp.einsum(
        "ne,de->nd", grad_rproj_low, proj_full, preferred_element_type=jnp.float32
    )
    grad_ratt = grad_ratt.astype(jnp.bfloat16).reshape(1, regions_dev, head_count, HEAD_DIM)
    grad_rq, grad_rk, grad_rv = attend_backward(
        heads_q, heads_k, heads_v, region_lse, grad_ratt, allowed
    )
    near_grad = jnp.concatenate(
        [grad_rk.reshape(near_count, model_width), grad_rv.reshape(near_count, model_width)], axis=1
    )
    own_grad = near_grad[span_dev * regions_dev : (span_dev + 1) * regions_dev]
    for offset in range(-span_dev, span_dev + 1):
        if offset != 0:
            outgoing = near_grad[
                (offset + span_dev) * regions_dev : (offset + span_dev + 1) * regions_dev
            ]
            own_grad = own_grad + shifted_2(
                outgoing.astype(jnp.bfloat16), ("dp", "fsdp"), offset
            ).astype(outgoing.dtype)
    grad_rmixed = jnp.concatenate(
        [grad_rq.reshape(regions_dev, model_width), own_grad], axis=1
    ).astype(jnp.bfloat16)
    grad_qkv = grad_qkv + jnp.einsum(
        "nd,ne->de", region_low, grad_rmixed, preferred_element_type=jnp.float32
    )
    grad_bias_q = grad_bias_q + jnp.sum(grad_rmixed[:, :model_width].astype(jnp.float32), axis=0)
    grad_bias_v = grad_bias_v + jnp.sum(
        grad_rmixed[:, 2 * model_width :].astype(jnp.float32), axis=0
    )
    grad_rnorm = jnp.einsum("ne,de->nd", grad_rmixed, qkv_full, preferred_element_type=jnp.float32)
    grad_region, grad_gain_zero, grad_shift_zero = norm_backward(
        grad_rnorm, region_hat, region_std, gain_full[0]
    )
    grad_regional = (grad_region + grad_region_mid).astype(jnp.bfloat16)
    grad_gains = jnp.stack([grad_gain_zero, grad_gain_one, grad_gain_two])
    grad_biases = jnp.concatenate(
        [
            jnp.stack(
                [
                    grad_shift_zero,
                    grad_shift_one,
                    grad_shift_two,
                    grad_bias_q,
                    grad_bias_v,
                    grad_bias_proj,
                ]
            ),
            grad_bias_up.reshape(-1, model_width),
            grad_bias_down[None],
        ],
        axis=0,
    )
    grad_qkv, grad_proj, grad_up, grad_down, grad_gains, grad_biases = (
        lax.psum_scatter(
            grad_qkv.astype(jnp.bfloat16), "fsdp", scatter_dimension=0, tiled=True
        ).astype(jnp.float32),
        lax.psum_scatter(
            grad_proj.astype(jnp.bfloat16), "fsdp", scatter_dimension=0, tiled=True
        ).astype(jnp.float32),
        lax.psum_scatter(
            grad_up.astype(jnp.bfloat16), "fsdp", scatter_dimension=0, tiled=True
        ).astype(jnp.float32),
        lax.psum_scatter(
            grad_down.astype(jnp.bfloat16), "fsdp", scatter_dimension=0, tiled=True
        ).astype(jnp.float32),
        lax.psum_scatter(
            grad_gains.astype(jnp.bfloat16), "fsdp", scatter_dimension=1, tiled=True
        ).astype(jnp.float32),
        lax.psum_scatter(
            grad_biases.astype(jnp.bfloat16), "fsdp", scatter_dimension=1, tiled=True
        ).astype(jnp.float32),
    )
    grad_qkv, grad_proj, grad_up, grad_down = (
        lax.psum_scatter(
            grad_qkv.astype(jnp.bfloat16), "dp", scatter_dimension=1, tiled=True
        ).astype(jnp.float32),
        lax.psum_scatter(
            grad_proj.astype(jnp.bfloat16), "dp", scatter_dimension=1, tiled=True
        ).astype(jnp.float32),
        lax.psum_scatter(
            grad_up.astype(jnp.bfloat16), "dp", scatter_dimension=1, tiled=True
        ).astype(jnp.float32),
        lax.psum_scatter(
            grad_down.astype(jnp.bfloat16), "dp", scatter_dimension=1, tiled=True
        ).astype(jnp.float32),
    )
    grad_gains, grad_biases = lax.psum((grad_gains, grad_biases), "dp")
    return (
        out_regional,
        out_local,
        grad_regional,
        grad_local,
        grad_qkv,
        grad_proj,
        grad_up,
        grad_down,
        grad_gains,
        grad_biases,
    )


def solution(mesh):
    in_specs = (
        P(("dp", "fsdp"), None),
        P(("dp", "fsdp"), None, None),
        P("fsdp", "dp"),
        P("fsdp", "dp"),
        P("fsdp", "dp"),
        P("fsdp", "dp"),
        P(None, "fsdp"),
        P(None, "fsdp"),
        P(),
        P(("dp", "fsdp"), None),
        P(("dp", "fsdp"), None, None),
    )
    out_specs = (
        P(("dp", "fsdp"), None),
        P(("dp", "fsdp"), None, None),
        P(("dp", "fsdp"), None),
        P(("dp", "fsdp"), None, None),
        P("fsdp", "dp"),
        P("fsdp", "dp"),
        P("fsdp", "dp"),
        P("fsdp", "dp"),
        P(None, "fsdp"),
        P(None, "fsdp"),
    )
    return jax.shard_map(
        on_device, mesh=mesh, in_specs=in_specs, out_specs=out_specs, check_vma=False
    )
```

profile of v0, /device:TPU:0, one launch (start us, length us, event | category | flops | bytes accessed | tf_op | source)
XLA Modules:
  0.0 1194.4 jit_solution(10371840208688339401)
XLA Ops:
  18.6 43.1 %all-gather.1 = bf16[16,32,11]{1,2,0:T(8,128)(2,1)S(1)} all-gather(bf16[1,32,11]{1,2,0:T(8,128)(2,1)} %bitcast.189), channel_id=1, replica_groups=mesh['dp'=2,'fsdp'=16] {'fsdp'}, dimensions={0}, use_global_device_ids=true | all-gather | bytes 11968 | tf_op jit(solution)/shard_map/all_gather | solution.py:101
  64.4 35.8 %all-gather = bf16[16,32,3]{1,2,0:T(4,128)(2,1)S(1)} all-gather(bf16[1,32,3]{1,2,0:T(4,128)(2,1)} %bitcast.195), channel_id=1, replica_groups=mesh['dp'=2,'fsdp'=16] {'fsdp'}, dimensions={0}, use_global_device_ids=true | all-gather | bytes 3264 | tf_op jit(solution)/shard_map/all_gather | solution.py:100
  103.7 42.2 %all_gather.44 = bf16[512,512]{1,0:T(8,128)(2,1)S(1)} all-gather(bf16[32,512]{1,0:T(8,128)(2,1)S(1)} %all_gather.43), channel_id=1, replica_groups=mesh['dp'=2,'fsdp'=16] {'fsdp'}, dimensions={0}, use_global_device_ids=true | all-gather | bytes 557056 | tf_op jit(solution)/shard_map/all_gather | solution.py:99
  186.5 7.7 copy.200
  194.2 5.5 reshape.393
  199.7 6.6 fusion.72
  211.1 11.8 reshape.423
  222.9 13.9 %copy.206 = bf16[48,50,16,32]{1,3,2,0:T(8,128)(2,1)} copy(bf16[48,50,16,32]{3,2,1,0:T(8,128)(2,1)} %reshape.423) | data formatting | bytes 4915200 | tf_op jit(solution)/shard_map/reshape | solution.py:178
  236.8 11.8 reshape.424
  248.6 13.9 %copy.207 = bf16[48,50,16,32]{1,3,2,0:T(8,128)(2,1)} copy(bf16[48,50,16,32]{3,2,1,0:T(8,128)(2,1)} %reshape.424) | data formatting | bytes 4915200 | tf_op jit(solution)/shard_map/reshape | solution.py:179
  262.5 8.2 reshape.422
  270.7 14.4 %copy.208 = bf16[48,50,16,32]{1,3,2,0:T(8,128)(2,1)} copy(bf16[48,50,16,32]{3,2,1,0:T(8,128)(2,1)} %reshape.422) | data formatting | bytes 4915200 | tf_op jit(solution)/shard_map/reshape | solution.py:180
  285.1 13.3 %multiply_reduce_fusion.1 = (f32[48,16,50]{2,1,0:T(8,128)S(1)}, f32[48,16,50,50]{2,3,1,0:T(8,128)}) fusion(bf16[48,50,16,32]{1,3,2,0:T(8,128)(2,1)} %copy.206, bf16[48,50,16,32]{1,3,2,0:T(8,128)(2,1)} %copy.207), kind=kOutput, calls=%fused_computation.23 | convolution fusion | flops 126681600 | bytes 12748800 | tf_op jit(solution)/shard_map/bqhe,bkhe->bhqk/dot_general | solution.py:48
  298.4 10.8 fusion.6
  310.1 14.3 %convert_bitcast_fusion.1 = bf16[48,50,16,32]{1,3,2,0:T(8,128)(2,1)} fusion(bf16[48,50,16,32]{1,3,2,0:T(8,128)(2,1)} %copy.208, f32[48,16,50,50]{2,3,1,0:T(8,128)} %get-tuple-element.107, f32[48,16,50]{2,1,0:T(8,128)S(1)} %fusion.6, f32[48,16,50]{2,1,0:T(8,128)S(1)} %get-tuple-element.106), kind=kOutput, calls=%fused_computation.34 | convolution fusion | flops 131788800 | bytes 12902400 | tf_op jit(solution)/shard_map/bhqk,bkhe->bqhe/dot_general | solution.py:62
  324.4 9.5 copy.210
  333.9 8.3 reshape.397
  350.4 52.3 %multiply_convert_fusion.1 = (bf16[2400,2048]{1,0:T(8,128)(2,1)}, f32[2400,2048]{1,0:T(8,128)}, f32[2400,2048]{1,0:T(8,128)}) fusion(f32[2048]{0:T(1024)S(1)} %bitcast.187, bf16[512,2048]{1,0:T(8,128)(2,1)} %all-gather.8.cloned.1.call-done, f32[2400,512]{1,0:T(8,128)} %copy-done.1, f32[512]{0:T(512)S(1)} %bitcast.191, f32[512]{0:T(512)S(1)} %bitcast.177, ...), kind=kOutput, calls=%fused_computation.8 | convolution fusion | flops 5363712000 | bytes 56195840 | tf_op jit(solution)/shard_map/dot_general | solution.py:187
  402.7 22.8 %fusion.81 = (bf16[2048]{0:T(1024)(128)(2,1)}, bf16[2400,2048]{1,0:T(8,128)(2,1)}) fusion(f32[2400,2048]{1,0:T(8,128)} %get-tuple-element.77, bf16[2400,512]{1,0:T(8,128)(2,1)S(1)} %copy-done.12, bf16[2048,512]{1,0:T(8,128)(2,1)} %all-gather.10.cloned.1.call-done, f32[2400,2048]{1,0:T(8,128)} %get-tuple-element.110, f32[2048]{0:T(1024)S(1)} %bitcast.188), kind=kOutput, calls=%fused_computation.190 | convolution fusion | flops 5111805952 | bytes 53719040 | tf_op jit(solution)/shard_map/nd,fd->nf/dot_general | solution.py:204
  425.5 12.3 %multiply_reduce_fusion.2 = (bf16[512]{0:T(512)(128)(2,1)}, f32[2400]{0:T(1024)S(1)}, f32[2400]{0:T(1024)S(1)}, bf16[512]{0:T(512)(128)(2,1)}, f32[2400,512]{1,0:T(8,128)S(1)}) fusion(f32[2400,512]{1,0:T(8,128)S(1)} %copy-done.2, f32[2400]{0:T(1024)S(1)} %add_rsqrt_fusion.1, f32[2400]{0:T(1024)S(1)} %broadcast_multiply_fusion.5, f32[512]{0:T(512)S(1)} %bitcast.178, ...), kind=kOutput, calls=%fused_computation.46 | convolution fusion | flops 5044217856 | bytes 21800448 | tf_op jit(solution)/shard_map/nf,df->nd/dot_general | solution.py:208
  444.7 8.1 reshape.425
  452.8 14.0 %copy.213 = bf16[48,50,16,32]{1,3,2,0:T(8,128)(2,1)} copy(bf16[48,50,16,32]{3,2,1,0:T(8,128)(2,1)} %reshape.425) | data formatting | bytes 4915200 | tf_op jit(solution)/shard_map/reshape | solution.py:218
  466.8 14.0 %convert_bitcast_fusion = bf16[48,50,16,32]{1,3,2,0:T(8,128)(2,1)} fusion(bf16[48,50,16,32]{1,3,2,0:T(8,128)(2,1)} %copy.213, f32[48,16,50,50]{2,3,1,0:T(8,128)} %get-tuple-element.107, f32[48,16,50]{2,1,0:T(8,128)S(1)} %copy-done.15), kind=kOutput, calls=%fused_computation.33 | convolution fusion | flops 129868800 | bytes 12748800 | tf_op jit(solution)/shard_map/bhqk,bqhe->bkhe/dot_general | solution.py:70
  480.8 23.0 %multiply_reduce_fusion = (f32[48,16,50]{2,1,0:T(8,128)S(1)}, f32[48,16,50,50]{2,3,1,0:T(8,128)}) fusion(f32[48,16,50,50]{2,3,1,0:T(8,128)} %get-tuple-element.107, f32[48,16,50]{2,1,0:T(8,128)S(1)} %copy-done.15, bf16[48,50,16,32]{1,3,2,0:T(8,128)(2,1)} %copy.213, bf16[48,50,16,32]{1,3,2,0:T(8,128)(2,1)} %copy.208), kind=kOutput, calls=%fused_computation.2 | convolution fusion | flops 130521600 | bytes 20582400 | tf_op jit(solution)/shard_map/bqhe,bkhe->bhqk/dot_general | solution.py:73
  503.8 19.1 %multiply_convert_fusion = bf16[48,16,50,50]{2,3,1,0:T(8,128)(2,1)} fusion(f32[48,16,50,50]{2,3,1,0:T(8,128)} %get-tuple-element.113, f32[48,16,50,50]{2,3,1,0:T(8,128)} %get-tuple-element.107, f32[48,16,50]{2,1,0:T(8,128)S(1)} %get-tuple-element.112, f32[48,16,50]{2,1,0:T(8,128)S(1)} %copy-done.15), kind=kLoop, calls=%fused_computation.1 | loop fusion | flops 9600000 | bytes 19507200 | tf_op jit(solution)/shard_map/convert_element_type | solution.py:79
  523.0 10.3 fusion.14
  533.2 11.9 fusion.13
  545.1 9.5 copy.223
  554.6 8.3 reshape.404
  562.9 10.3 copy.217
  573.2 9.2 reshape.402
  582.5 9.5 copy.220
  592.0 9.6 reshape.403
  606.4 6.4 multiply_reduce_fusion.3
  616.5 5.5 reshape.405
  634.9 11.4 fusion.71
  646.3 7.6 collective-permute-start.11
  676.3 10.9 convolution_convert_fusion.1
  687.5 12.6 %convolution_convert_fusion.2 = bf16[512,2048]{1,0:T(8,128)(2,1)} fusion(bf16[2400,2048]{1,0:T(8,128)(2,1)} %get-tuple-element.119, f32[2400,512]{1,0:T(8,128)} %copy-done.1, f32[512]{0:T(512)S(1)} %bitcast.192, f32[512]{0:T(512)S(1)} %bitcast.180, f32[2400]{0:T(1024)S(1)} %copy-done.42, f32[2400]{0:T(1024)S(1)} %copy-done.37), kind=kOutput, calls=%fused_computation.66 | convolution fusion | flops 5040357376 | bytes 16866048 | tf_op jit(solution)/shard_map/nd,nf->df/dot_general | solution.py:206
  709.4 124.1 %reduce-scatter.15.cloned.1.call-done = bf16[32,1536]{1,0:T(8,128)(2,1)} async-done(((bf16[512,1536]{1,0:T(8,128)(2,1)}), bf16[32,1536]{1,0:T(8,128)(2,1)}) %reduce-scatter.15.cloned.1.call-update) | async-done | bytes 98320 | tf_op jit(solution)/shard_map/reduce_scatter | solution.py:298
  833.6 82.2 %reduce-scatter.27.cloned.1.call-done = bf16[128,512]{1,0:T(8,128)(2,1)} async-done(((bf16[2048,512]{1,0:T(8,128)(2,1)}), bf16[128,512]{1,0:T(8,128)(2,1)}) %reduce-scatter.27.cloned.1.call-update) | async-done | bytes 131088 | tf_op jit(solution)/shard_map/reduce_scatter | solution.py:307
  916.1 80.3 %reduce-scatter.23.cloned.1.call-done = bf16[32,2048]{1,0:T(8,128)(2,1)} async-done(((bf16[512,2048]{1,0:T(8,128)(2,1)}), bf16[32,2048]{1,0:T(8,128)(2,1)}) %reduce-scatter.23.cloned.1.call-update) | async-done | bytes 131088 | tf_op jit(solution)/shard_map/reduce_scatter | solution.py:304
  996.5 10.3 add_convert_fusion.1
  1019.9 52.4 %reduce-scatter.31.cloned.1.call-done = bf16[32,3]{1,0:T(8,128)(2,1)} async-done(((bf16[512,3]{1,0:T(8,128)(2,1)}), bf16[32,3]{1,0:T(8,128)(2,1)}) %reduce-scatter.31.cloned.1.call-update) | async-done | bytes 208
  1073.1 74.2 %reduce-scatter.33.cloned.1.call-done = bf16[32,11]{1,0:T(8,128)(2,1)} async-done(((bf16[512,11]{1,0:T(8,128)(2,1)}), bf16[32,11]{1,0:T(8,128)(2,1)}) %reduce-scatter.33.cloned.1.call-update) | async-done | bytes 720
  1154.6 9.6 reduce-scatter.17.cloned.1.call-done
  1165.7 9.4 reduce-scatter.29.cloned.1.call-done
  1176.6 9.5 reduce-scatter.25.cloned.1.call-done
  (334 shorter events, 156.9 us)
Async XLA Ops:
  7.2 142.1 %copy-start.14 = (bf16[48,49,512]{2,0,1:T(8,128)(2,1)S(1)}, bf16[48,49,512]{2,0,1:T(8,128)(2,1)}, u32[]{:S(2)}) copy-start(bf16[48,49,512]{2,0,1:T(8,128)(2,1)} %param.21) | copy-start | bytes 7225348
  7.2 138.7 %all-gather.6.cloned.1.call-start = ((), (), s32[]{:S(2)}) async-start(), calls=%async_computation.10 | async-start | bytes 1671168 | tf_op jit(solution)/shard_map/all_gather | solution.py:98
  11.1 339.2 %all-gather.8.cloned.1.call-start = ((), (), s32[]{:S(2)}) async-start(), calls=%async_computation.11 | async-start | bytes 2228224 | tf_op jit(solution)/shard_map/all_gather | solution.py:112
  14.7 387.9 %all-gather.10.cloned.1.call-start = ((), (), s32[]{:S(2)}) async-start(), calls=%async_computation.12 | async-start | bytes 2228224 | tf_op jit(solution)/shard_map/all_gather | solution.py:113
  18.6 690.3 %reduce-scatter.19.cloned.1.call-start = ((), (), s32[]{:S(2)}) async-start(), calls=%async_computation.15 | async-start | bytes 557056 | tf_op jit(solution)/shard_map/reduce_scatter | solution.py:301
  62.4 85.5 %copy-start.47 = (f32[1,512]{1,0:T(1,128)}, f32[1,512]{1,0:T(1,128)S(1)}, u32[]{:S(2)}) copy-start(f32[1,512]{1,0:T(1,128)S(1)} %get-tuple-element.100) | copy-start | bytes 6148
  62.4 137.3 %copy-start.62 = (f32[1,512]{1,0:T(1,128)}, f32[1,512]{1,0:T(1,128)S(1)}, u32[]{:S(2)}) copy-start(f32[1,512]{1,0:T(1,128)S(1)} %get-tuple-element.96) | copy-start | bytes 6148
  62.4 287.9 %copy-start.60 = (f32[1,512]{1,0:T(1,128)}, f32[1,512]{1,0:T(1,128)S(1)}, u32[]{:S(2)}) copy-start(f32[1,512]{1,0:T(1,128)S(1)} %get-tuple-element.95) | copy-start | bytes 6148
  63.4 84.5 %copy-start.49 = (f32[48]{0:T(128)}, f32[48]{0:T(128)S(1)}, u32[]{:S(2)}) copy-start(f32[48]{0:T(128)S(1)} %broadcast_multiply_fusion.8) | copy-start | bytes 580
  64.4 83.5 %copy-start.51 = (f32[48]{0:T(128)}, f32[48]{0:T(128)S(1)}, u32[]{:S(2)}) copy-start(f32[48]{0:T(128)S(1)} %add_rsqrt_fusion.2) | copy-start | bytes 580
  100.3 53.0 %copy-start.39 = (f32[1,512]{1,0:T(1,128)}, f32[1,512]{1,0:T(1,128)S(1)}, u32[]{:S(2)}) copy-start(f32[1,512]{1,0:T(1,128)S(1)} %get-tuple-element.103) | copy-start | bytes 6148
  100.3 99.4 %copy-start.56 = (f32[1,512]{1,0:T(1,128)}, f32[1,512]{1,0:T(1,128)S(1)}, u32[]{:S(2)}) copy-start(f32[1,512]{1,0:T(1,128)S(1)} %get-tuple-element.102) | copy-start | bytes 6148
  100.3 337.5 %copy-start.54 = (f32[1,512]{1,0:T(1,128)}, f32[1,512]{1,0:T(1,128)S(1)}, u32[]{:S(2)}) copy-start(f32[1,512]{1,0:T(1,128)S(1)} %get-tuple-element.101) | copy-start | bytes 6148
  145.8 196.3 %copy-start.10 = (bf16[512,512]{1,0:T(8,128)(2,1)}, bf16[512,512]{1,0:T(8,128)(2,1)S(1)}, u32[]{:S(2)}) copy-start(bf16[512,512]{1,0:T(8,128)(2,1)S(1)} %all_gather.44) | copy-start | bytes 1572868
  148.0 21.1 %collective-permute-start = (bf16[48,1024]{1,0:T(8,128)(2,1)S(1)}, bf16[48,1024]{1,0:T(8,128)(2,1)S(1)}, u32[]{:S(2)}, u32[]{:S(2)}) collective-permute-start(bf16[48,1024]{1,0:T(8,128)(2,1)S(1)} %pad_maximum_fusion.4), channel_id=1, source_target_pairs={{0,3},{1,4},{2,5},{3,6},{4,7},{5,8},{6,9},{7,10},{8,11},{9,12},{10... | collective-permute-start | bytes 294920 | tf_op jit(solution)/shard_map/ppermute | solution.py:19
  160.5 17.0 %collective-permute-start.5 = (bf16[48,1024]{1,0:T(8,128)(2,1)S(1)}, bf16[48,1024]{1,0:T(8,128)(2,1)S(1)}, u32[]{:S(2)}, u32[]{:S(2)}) collective-permute-start(bf16[48,1024]{1,0:T(8,128)(2,1)S(1)} %pad_maximum_fusion.4), channel_id=1, source_target_pairs={{3,0},{4,1},{5,2},{6,3},{7,4},{8,5},{9,6},{10,7},{11,8},{12,9},{13... | collective-permute-start | bytes 294920 | tf_op jit(solution)/shard_map/ppermute | solution.py:19
  161.8 15.7 %collective-permute-start.4 = (bf16[48,1024]{1,0:T(8,128)(2,1)S(1)}, bf16[48,1024]{1,0:T(8,128)(2,1)S(1)}, u32[]{:S(2)}, u32[]{:S(2)}) collective-permute-start(bf16[48,1024]{1,0:T(8,128)(2,1)S(1)} %pad_maximum_fusion.4), channel_id=1, source_target_pairs={{2,0},{3,1},{4,2},{5,3},{6,4},{7,5},{8,6},{9,7},{10,8},{11,9},{12,... | collective-permute-start | bytes 294920 | tf_op jit(solution)/shard_map/ppermute | solution.py:19
  163.1 14.3 %collective-permute-start.3 = (bf16[48,1024]{1,0:T(8,128)(2,1)S(1)}, bf16[48,1024]{1,0:T(8,128)(2,1)S(1)}, u32[]{:S(2)}, u32[]{:S(2)}) collective-permute-start(bf16[48,1024]{1,0:T(8,128)(2,1)S(1)} %pad_maximum_fusion.4), channel_id=1, source_target_pairs={{1,0},{2,1},{3,2},{4,3},{5,4},{6,5},{7,6},{8,7},{9,8},{10,9},{11,1... | collective-permute-start | bytes 294920 | tf_op jit(solution)/shard_map/ppermute | solution.py:19
  164.4 13.0 %collective-permute-start.2 = (bf16[48,1024]{1,0:T(8,128)(2,1)S(1)}, bf16[48,1024]{1,0:T(8,128)(2,1)S(1)}, u32[]{:S(2)}, u32[]{:S(2)}) collective-permute-start(bf16[48,1024]{1,0:T(8,128)(2,1)S(1)} %pad_maximum_fusion.4), channel_id=1, source_target_pairs={{0,1},{1,2},{2,3},{3,4},{4,5},{5,6},{6,7},{7,8},{8,9},{9,10},{10,1... | collective-permute-start | bytes 294920 | tf_op jit(solution)/shard_map/ppermute | solution.py:19
  169.1 8.3 collective-permute-start.1
  347.1 90.7 %copy-start.36 = (f32[2400]{0:T(1024)}, f32[2400]{0:T(1024)S(1)}, u32[]{:S(2)}) copy-start(f32[2400]{0:T(1024)S(1)} %broadcast_multiply_fusion.5) | copy-start | bytes 28804
  350.3 87.5 %copy-start.41 = (f32[2400]{0:T(1024)}, f32[2400]{0:T(1024)S(1)}, u32[]{:S(2)}) copy-start(f32[2400]{0:T(1024)S(1)} %add_rsqrt_fusion.1) | copy-start | bytes 28804
  350.4 52.3 %copy-start.12 = (bf16[2400,512]{1,0:T(8,128)(2,1)S(1)}, bf16[2400,512]{1,0:T(8,128)(2,1)}, u32[]{:S(2)}) copy-start(bf16[2400,512]{1,0:T(8,128)(2,1)} %reshape.399) | copy-start | bytes 7372804
  466.8 56.1 %slice-start = ((s8[6291456]{0:T(1024)(128)(4,1)}), s8[2097152]{0:T(1024)(128)(4,1)S(1)}, s32[]{:S(2)}) async-start(s8[6291456]{0:T(1024)(128)(4,1)} %bitcast.139), calls=%async_computation.23 | async-start | bytes 4194304
  480.8 42.1 %slice-start.1 = ((s8[6291456]{0:T(1024)(128)(4,1)}), s8[4194304]{0:T(1024)(128)(4,1)S(1)}, s32[]{:S(2)}) async-start(s8[6291456]{0:T(1024)(128)(4,1)} %bitcast.139), calls=%async_computation.24 | async-start | bytes 8388608
  562.9 43.0 %copy-start.6 = (bf16[2400,512]{0,1:T(8,128)(2,1)}, bf16[2400,512]{0,1:T(8,128)(2,1)S(1)}, u32[]{:S(2)}) copy-start(bf16[2400,512]{0,1:T(8,128)(2,1)S(1)} %reshape.404) | copy-start | bytes 7372804
  627.8 205.7 %reduce-scatter.15.cloned.1.call-start = ((), (), s32[]{:S(2)}) async-start(), calls=%async_computation.13 | async-start | bytes 1671168 | tf_op jit(solution)/shard_map/reduce_scatter | solution.py:298
  633.3 31.5 %copy-start.22 = (bf16[336,512]{0,1:T(8,128)(2,1)S(1)}, bf16[336,512]{0,1:T(8,128)(2,1)}, u32[]{:S(2)}) copy-start(bf16[336,512]{0,1:T(8,128)(2,1)} %copy-done.21) | copy-start | bytes 1032196
  633.3 39.0 %copy-start.24 = (bf16[48,512]{1,0:T(8,128)(2,1)S(1)}, bf16[48,512]{1,0:T(8,128)(2,1)}, u32[]{:S(2)}) copy-start(bf16[48,512]{1,0:T(8,128)(2,1)} %param.11) | copy-start | bytes 147460
  633.3 39.0 %copy-start.40 = (f32[1,512]{1,0:T(1,128)S(1)}, f32[1,512]{1,0:T(1,128)}, u32[]{:S(2)}) copy-start(f32[1,512]{1,0:T(1,128)} %copy-done.39) | copy-start | bytes 6148
  633.3 39.1 %copy-start.48 = (f32[1,512]{1,0:T(1,128)S(1)}, f32[1,512]{1,0:T(1,128)}, u32[]{:S(2)}) copy-start(f32[1,512]{1,0:T(1,128)} %copy-done.47) | copy-start | bytes 6148
  633.3 39.1 %copy-start.50 = (f32[48]{0:T(128)S(1)}, f32[48]{0:T(128)}, u32[]{:S(2)}) copy-start(f32[48]{0:T(128)} %copy-done.49) | copy-start | bytes 580
  633.3 39.1 %copy-start.52 = (f32[48]{0:T(128)S(1)}, f32[48]{0:T(128)}, u32[]{:S(2)}) copy-start(f32[48]{0:T(128)} %copy-done.51) | copy-start | bytes 580
  633.3 29.8 %collective-permute-start.6 = (bf16[48,1024]{1,0:T(8,128)(2,1)S(1)}, bf16[48,1024]{1,0:T(8,128)(2,1)S(1)}, u32[]{:S(2)}, u32[]{:S(2)}) collective-permute-start(bf16[48,1024]{1,0:T(8,128)(2,1)S(1)} %get-tuple-element.82), channel_id=1, source_target_pairs={{3,0},{4,1},{5,2},{6,3},{7,4},{8,5},{9,6},{10,7},{11,8},{12,9},{13... | collective-permute-start | bytes 294920 | tf_op jit(solution)/shard_map/ppermute | solution.py:19
  646.3 20.6 %collective-permute-start.11 = (bf16[48,1024]{1,0:T(8,128)(2,1)}, bf16[48,1024]{1,0:T(8,128)(2,1)}, u32[]{:S(2)}, u32[]{:S(2)}) collective-permute-start(bf16[48,1024]{1,0:T(8,128)(2,1)} %get-tuple-element.83), channel_id=1, source_target_pairs={{0,3},{1,4},{2,5},{3,6},{4,7},{5,8},{6,9},{7,10},{8,11},{9,12},{10... | collective-permute-start | bytes 294920 | tf_op jit(solution)/shard_map/ppermute | solution.py:19
  653.9 12.9 %collective-permute-start.10 = (bf16[48,1024]{1,0:T(8,128)(2,1)}, bf16[48,1024]{1,0:T(8,128)(2,1)}, u32[]{:S(2)}, u32[]{:S(2)}) collective-permute-start(bf16[48,1024]{1,0:T(8,128)(2,1)} %get-tuple-element.84), channel_id=1, source_target_pairs={{0,2},{1,3},{2,4},{3,5},{4,6},{5,7},{6,8},{7,9},{8,10},{9,11},{10,... | collective-permute-start | bytes 294920 | tf_op jit(solution)/shard_map/ppermute | solution.py:19
  659.1 7.8 collective-permute-start.9
  661.8 7.5 collective-permute-start.8
  663.2 7.9 collective-permute-start.7
  676.2 239.6 %reduce-scatter.27.cloned.1.call-start = ((), (), s32[]{:S(2)}) async-start(), calls=%async_computation.19 | async-start | bytes 2228224 | tf_op jit(solution)/shard_map/reduce_scatter | solution.py:307
  687.2 309.2 %reduce-scatter.23.cloned.1.call-start = ((), (), s32[]{:S(2)}) async-start(), calls=%async_computation.17 | async-start | bytes 2228224 | tf_op jit(solution)/shard_map/reduce_scatter | solution.py:304
  700.1 372.2 %reduce-scatter.31.cloned.1.call-start = ((), (), s32[]{:S(2)}) async-start(), calls=%async_computation.21 | async-start | bytes 139264
  700.2 296.3 %copy-start.59 = (f32[1,512]{1,0:T(1,128)S(1)}, f32[1,512]{1,0:T(1,128)}, u32[]{:S(2)}) copy-start(f32[1,512]{1,0:T(1,128)} %get-tuple-element.94) | copy-start | bytes 6148
  707.0 440.4 %reduce-scatter.33.cloned.1.call-start = ((), (), s32[]{:S(2)}) async-start(), calls=%async_computation.22 | async-start | bytes 139264
  708.7 444.5 %reduce-scatter.21.cloned.1.call-start = ((), (), s32[]{:S(2)}) async-start(), calls=%async_computation.16 | async-start | bytes 49152 | tf_op jit(solution)/shard_map/reduce_scatter | solution.py:321
  709.3 454.9 %reduce-scatter.17.cloned.1.call-start = ((), (), s32[]{:S(2)}) async-start(), calls=%async_computation.14 | async-start | bytes 147456 | tf_op jit(solution)/shard_map/reduce_scatter | solution.py:318
  833.5 341.6 %reduce-scatter.29.cloned.1.call-start = ((), (), s32[]{:S(2)}) async-start(), calls=%async_computation.20 | async-start | bytes 196608 | tf_op jit(solution)/shard_map/reduce_scatter | solution.py:327
  915.8 270.2 %reduce-scatter.25.cloned.1.call-start = ((), (), s32[]{:S(2)}) async-start(), calls=%async_computation.18 | async-start | bytes 196608 | tf_op jit(solution)/shard_map/reduce_scatter | solution.py:324
  (49 other events, 371.9 us)
Sparse Core Ops, SparseCore 0:
  11.2 60.3 all-gather.5
  74.4 63.0 all-gather.7
  140.3 61.3 all-gather.9
  627.9 79.0 reduce-scatter.18
  712.4 121.0 reduce-scatter.14
  836.3 79.4 reduce-scatter.26
  918.7 77.6 reduce-scatter.22
  999.3 72.9 reduce-scatter.30
  1075.1 72.1 reduce-scatter.32
  1149.5 3.7 reduce-scatter.20
  1155.5 8.6 reduce-scatter.16
  1166.4 8.6 reduce-scatter.28
  1177.4 8.6 reduce-scatter.24
where the time goes:
time: 1200 us; the launch traced here: 1190 us
  waiting for transfers between devices  452 us (38%)
  matrix products  256 us (21%)
  local copies, waits for them, and re-layouts  230 us (19%)
  blocking collectives  138 us (12%)
  other arithmetic  68 us (6%)
  starting transfers between devices  35.3 us (3%)
  between operations  15.7 us (1%)
    unnamed x15, waiting for transfers between devices  127 us
    reduce_scatter x1, waiting for transfers between devices, on_device(): lax.psum_scatter(grad_qkv.astype(jnp.bfloat16), 'fsdp', scatter_dimension...  124 us
    reduce_scatter x1, waiting for transfers between devices, on_device(): lax.psum_scatter(grad_down.astype(jnp.bfloat16), 'fsdp', scatter_dimensio...  82.2 us
    reduce_scatter x1, waiting for transfers between devices, on_device(): lax.psum_scatter(grad_up.astype(jnp.bfloat16), 'fsdp', scatter_dimension=...  80.3 us
    dot_general x1, matrix products, on_device(): jnp.dot(low_two, up_full, preferred_element_type=jnp.float32) + bias_up  52.3 us
    all_gather x1, blocking collectives, fetch_attention(): lax.all_gather(biases, 'fsdp', axis=1, tiled=True)  43.1 us
    all_gather x1, blocking collectives, fetch_attention(): lax.all_gather(w_proj, 'fsdp', axis=0, tiled=True)  42.2 us
    all_gather x1, blocking collectives, fetch_attention(): lax.all_gather(gains, 'fsdp', axis=1, tiled=True)  35.8 us
  transfers between devices with their start and end apart: 25, of which 12 were waited for; matrix products, arithmetic and copies ran while one was open for 27% of the time, Pallas kernels for 0%

commit v1 on v0

v1 whole, which is shorter than its diff:
```python
import math
from functools import partial

import jax
import jax.numpy as jnp
from jax import lax
from jax.experimental import pallas as pl
from jax.experimental.pallas import tpu as pltpu
from jax.sharding import PartitionSpec as P

HEAD_DIM = 32
MAX_REGIONS = 144
EPSILON = 1e-05
NEGATIVE = -1e30
PITCH = 56
SLOT = 64
LANES = 128
GROUP = LANES // HEAD_DIM
EXP_SCALE = HEAD_DIM ** (-0.5) * math.log2(math.e)
FACTOR = HEAD_DIM ** (-0.5)
VMEM_BYTES = 60 * 1024 * 1024

ERFC_P = 0.42
ERFC = (
    0.23681994,
    0.23965002,
    0.19433459,
    0.27000812,
    -0.13287422,
    0.44318139,
    -0.32169076,
    0.07057076,
)

BF16 = jnp.bfloat16
F32 = jnp.float32


def dot_nn(a, b):
    return lax.dot_general(a, b, (((1,), (0,)), ((), ())), preferred_element_type=F32)


def dot_nt(a, b):
    return lax.dot_general(a, b, (((1,), (1,)), ((), ())), preferred_element_type=F32)


def dot_tn(a, b):
    return lax.dot_general(a, b, (((0,), (0,)), ((), ())), preferred_element_type=F32)


def normalise(x):
    centred = x - jnp.mean(x, axis=-1, keepdims=True)
    inv_std = lax.rsqrt(jnp.mean(centred * centred, axis=-1, keepdims=True) + EPSILON)
    return centred * inv_std, inv_std


def norm_back(dy, hat, inv_std, gain):
    scaled = dy * gain
    mean_s = jnp.mean(scaled, axis=-1, keepdims=True)
    mean_h = jnp.mean(scaled * hat, axis=-1, keepdims=True)
    return inv_std * (scaled - mean_s - hat * mean_h)


def head_masks(rows):
    lane = lax.broadcasted_iota(jnp.int32, (rows, LANES), 1) // HEAD_DIM
    return [jnp.where(lane == h, 1.0, 0.0).astype(BF16) for h in range(GROUP)]


def spread(x, masks, order=(0, 1, 2, 3)):
    return jnp.concatenate([x * masks[h] for h in order], axis=0)


def turn(p):
    both = jnp.concatenate([p[:, :LANES], p[:, LANES:]], axis=0).T
    return jnp.concatenate([both[:SLOT], both[SLOT:]], axis=1)


TURNED = (0, 2, 1, 3)


def gelu_pair(h):
    z = jnp.abs(h) * (ERFC_P * math.sqrt(0.5)) + 1.0
    t = pl.reciprocal(z, approx=True)
    poly = jnp.full_like(t, ERFC[-1])
    for c in ERFC[-2::-1]:
        poly = poly * t + c
    bell = jnp.exp2(h * h * (-0.5 * math.log2(math.e)))
    tail = (poly * t) * (bell * 0.5)
    cdf = jnp.where(h < 0, tail, 1.0 - tail)
    return h * cdf, cdf + h * (bell * (1.0 / math.sqrt(2.0 * math.pi)))


def build_windows(z_ref, local_ref, row_ref):
    count, local_len, _ = local_ref.shape
    for w in range(count):
        z_ref[w * PITCH : w * PITCH + local_len] = local_ref[w].astype(F32)
        z_ref[w * PITCH + local_len : w * PITCH + local_len + 1] = row_ref[w : w + 1].astype(F32)


def split_windows(z, local_ref, row_ref):
    count, local_len, _ = local_ref.shape
    for w in range(count):
        local_ref[w] = z[w * PITCH : w * PITCH + local_len].astype(local_ref.dtype)
        row_ref[w : w + 1] = z[w * PITCH + local_len : w * PITCH + local_len + 1].astype(row_ref.dtype)


def pack_weights_kernel(
    wqkv_ref, wproj_ref, gains_ref, biases_ref, up_ref, down_ref, att_ref, mlp_ref, small_s
):
    row = 0
    small_s[...] = jnp.zeros_like(small_s)
    count, lanes = gains_ref.shape
    small_s[:count, :lanes] = gains_ref[...].astype(F32)
    small_s[count : count + biases_ref.shape[0], :lanes] = biases_ref[...].astype(F32)
    for ref in (wqkv_ref, wproj_ref, None):
        if ref is None:
            att_ref[row : row + lanes] = small_s[...].T[:lanes].astype(BF16)
            row += lanes
            continue
        for c in range(0, ref.shape[1], LANES):
            att_ref[row : row + ref.shape[0]] = ref[:, c : c + LANES]
            row += ref.shape[0]
    row = 0
    cols = down_ref.shape[1]
    for c in range(0, up_ref.shape[1], cols):
        mlp_ref[row : row + up_ref.shape[0]] = up_ref[:, c : c + cols]
        row += up_ref.shape[0]
    mlp_ref[row:] = down_ref[...]


def block_places(place_ref, stacks, codes):
    order, far_peers = codes
    per = len(stacks) // far_peers
    for i, stack in enumerate(stacks):
        deep = stack.shape[0]
        for k in range(deep):
            yield stack, k, place_ref[0] ^ (i // per), place_ref[1] ^ order[i % per * deep + k]


def assemble_attention(place_ref, stacks, codes, wqkv_ref, wproj_ref, norms_ref, small_s):
    peers, far_peers = len(codes[0]), codes[1]
    rows = wproj_ref.shape[0] // peers
    parts = [wqkv_ref.shape[1] // far_peers // LANES, wproj_ref.shape[1] // far_peers // LANES]
    for stack, k, d, f in block_places(place_ref, stacks, codes):
        here = pl.ds(pl.multiple_of(f * rows, rows), rows)
        row = 0
        for count, ref in zip(parts, (wqkv_ref, wproj_ref)):
            for j in range(count):
                to = pl.multiple_of((d * count + j) * LANES, LANES)
                ref[here, pl.ds(to, LANES)] = stack[k, row : row + rows]
                row += rows
        small_s[here] = stack[k, row : row + rows].astype(F32)
    norms_ref[...] = small_s[...].T[: norms_ref.shape[0]]


def pair_offsets(place_ref, peers, span):
    linear = place_ref[0] * peers + place_ref[1]
    for d in range(1, span + 1):
        low = lax.rem(linear, 2 * d) < d
        yield jnp.where(low, d, -d)
        yield jnp.where(low, -d, d)


def region_forward_kernel(place_ref, kid_ref, qid_ref, *refs, near, stacks, codes):
    x_refs, refs = refs[:near], refs[near:]
    if stacks:
        stack_refs, refs = refs[:stacks], refs[stacks:]
        mid_ref, hat_ref, qkv_ref, p_ref, o_ref, wqkv_ref, wproj_ref, norms_ref, small_s, x_s = refs
        assemble_attention(place_ref, stack_refs, codes, wqkv_ref, wproj_ref, norms_ref, small_s)
        own = mid_ref.shape[0]
        span = near // 2
        x_s[span * own : (span + 1) * own] = x_refs[0][...].astype(F32)
        for ref, by in zip(x_refs[1:], pair_offsets(place_ref, len(codes[0]), span)):
            x_s[pl.ds(pl.multiple_of((span + by) * own, 8), own)] = ref[...].astype(F32)
        x = x_s[...]
    else:
        wqkv_ref, wproj_ref, norms_ref, mid_ref, hat_ref, qkv_ref, p_ref, o_ref = refs
        x = jnp.concatenate([r[...].astype(F32) for r in x_refs], axis=0)
    own, width = mid_ref.shape
    rows = x.shape[0]
    first = (rows - own) // 2
    hat, _ = normalise(x)
    u = (hat * norms_ref[0:1] + norms_ref[3:4]).astype(BF16)
    hat_ref[...] = hat.astype(BF16)
    qkv = dot_nn(u, wqkv_ref[...])
    q = (qkv[:, :width] + norms_ref[6:7]).astype(BF16)
    k = qkv[:, width : 2 * width].astype(BF16)
    v = (qkv[:, 2 * width :] + norms_ref[7:8]).astype(BF16)
    qkv_ref[:, :width] = q
    qkv_ref[:, width : 2 * width] = k
    qkv_ref[:, 2 * width :] = v
    masks = head_masks(SLOT)
    same = kid_ref[...] == qid_ref[...]
    lane = lax.broadcasted_iota(jnp.int32, (1, GROUP * SLOT), 1)
    asked = (lane % SLOT) < own
    out_masks = [m.astype(F32) for m in masks]
    for c in range(width // LANES):
        cols = slice(c * LANES, (c + 1) * LANES)
        qx = spread(q[first : first + SLOT, cols], masks)
        s = jnp.where(same, dot_nt(k[:, cols], qx), NEGATIVE)
        e = jnp.exp2((s - jnp.max(s, axis=0, keepdims=True)) * EXP_SCALE)
        total = jnp.sum(e, axis=0, keepdims=True)
        p = (e * jnp.where(asked, 1.0 / total, 0.0)).astype(BF16)
        p_ref[c] = p
        mixed = dot_tn(p, v[:, cols])
        o = sum(mixed[h * SLOT : (h + 1) * SLOT] * out_masks[h] for h in range(GROUP))
        o_ref[:, cols] = o[:own].astype(BF16)
    mid_ref[...] = x[first : first + own] + dot_nn(o_ref[...], wproj_ref[...]) + norms_ref[8:9]


def window_forward_kernel(
    local_ref,
    row_ref,
    wqkv_ref,
    wproj_ref,
    norms_ref,
    *refs,
):
    z1_ref, hat_ref, qkv_ref, p_ref, o_ref, tick_ref, z_s, qkv_s, o_s = refs[-9:]
    tick_ref[...] = jnp.zeros_like(tick_ref)
    rows, width = z_s.shape
    count, local_len, _ = local_ref.shape

    @pl.when(pl.program_id(0) == 0)
    def _():
        z_s[...] = jnp.zeros_like(z_s)
        qkv_s[rows:, :] = jnp.zeros((qkv_s.shape[0] - rows, qkv_s.shape[1]), F32)

    build_windows(z_s, local_ref, row_ref)
    hat, _ = normalise(z_s[...])
    u = (hat * norms_ref[1:2] + norms_ref[4:5]).astype(BF16)
    hat_ref[...] = hat.astype(BF16)
    qkv_s[:rows, :width] = dot_nn(u, wqkv_ref[:, :width]) + norms_ref[6:7]
    qkv_s[:rows, width : 2 * width] = dot_nn(u, wqkv_ref[:, width : 2 * width])
    qkv_s[:rows, 2 * width :] = dot_nn(u, wqkv_ref[:, 2 * width :]) + norms_ref[7:8]
    masks = head_masks(SLOT)
    is_key = lax.broadcasted_iota(jnp.int32, (SLOT, GROUP * SLOT), 0) <= local_len
    lane = lax.broadcasted_iota(jnp.int32, (1, GROUP * SLOT), 1)
    asked = (lane % SLOT) <= local_len

    def window(w):
        base = pl.multiple_of(w * PITCH, 8)
        spots = [c * LANES for c in range(width // LANES)]
        scores, values = [], []
        for at in spots:
            q = qkv_s[pl.ds(base, SLOT), at : at + LANES].astype(BF16)
            k = qkv_s[pl.ds(base, SLOT), width + at : width + at + LANES].astype(BF16)
            v = qkv_s[pl.ds(base, SLOT), 2 * width + at : 2 * width + at + LANES].astype(BF16)
            qkv_ref[w, :, at : at + LANES] = q
            qkv_ref[w, :, width + at : width + at + LANES] = k
            qkv_ref[w, :, 2 * width + at : 2 * width + at + LANES] = v
            scores.append(dot_nt(k, spread(q, masks)))
            values.append(v)
        probs = []
        for c, s in enumerate(scores):
            s = jnp.where(is_key, s, NEGATIVE)
            e = jnp.exp2((s - jnp.max(s, axis=0, keepdims=True)) * EXP_SCALE)
            total = jnp.sum(e, axis=0, keepdims=True)
            p = (e * jnp.where(asked, 1.0 / total, 0.0)).astype(BF16)
            p_ref[w, c] = p
            probs.append(turn(p))
        for at, p, v in zip(spots, probs, values):
            o = dot_nn(p, spread(v, masks, TURNED))
            o_s[pl.ds(base, PITCH), at : at + LANES] = o[:PITCH]

    def windows(i, carry):
        for j in range(2):
            window(2 * i + j)
        return carry

    lax.fori_loop(0, count // 2, windows, 0)
    o = o_s[...].astype(BF16)
    o_ref[...] = o
    z1_ref[...] = z_s[...] + dot_nn(o, wproj_ref[...]) + norms_ref[8:9]


def assemble_mlp(place_ref, block_refs, up_ref, down_ref):
    fsdp, tall, cols = block_refs[0].shape
    far = place_ref[0]
    up_rows = up_ref.shape[0] // fsdp
    down_rows = down_ref.shape[0] // fsdp
    parts = (tall - down_rows) // up_rows
    for f in range(fsdp):
        for d, blocks_ref in enumerate(block_refs):
            col = d ^ far
            for j in range(parts):
                at = pl.multiple_of((col * parts + j) * cols, LANES)
                up_ref[f * up_rows : (f + 1) * up_rows, pl.ds(at, cols)] = blocks_ref[
                    f, j * up_rows : (j + 1) * up_rows
                ]
            at = pl.multiple_of(col * cols, LANES)
            down_ref[f * down_rows : (f + 1) * down_rows, pl.ds(at, cols)] = blocks_ref[
                f, parts * up_rows :
            ]


def pack_mlp(place_ref, gup_s, gdown_s, outs):
    fsdp = outs[0].shape[0]
    far = place_ref[0]
    width, hidden = gdown_s.shape
    up_rows, up_cols = width // fsdp, hidden // len(outs)
    down_rows, down_cols = width // len(outs), hidden // fsdp
    parts = up_cols // LANES
    for r, out in enumerate(outs):
        d = r ^ far
        for f in range(fsdp):
            here = slice(f * up_rows, (f + 1) * up_rows)
            for j in range(parts):
                at = pl.multiple_of((d * parts + j) * LANES, LANES)
                out[f, j * up_rows : (j + 1) * up_rows] = gup_s[here, pl.ds(at, LANES)].astype(BF16)
            at = pl.multiple_of(d * down_rows, 8)
            out[f, parts * up_rows :] = gdown_s[
                pl.ds(at, down_rows), f * down_cols : (f + 1) * down_cols
            ].astype(BF16)


def mlp_kernel(place_ref, z_ref, cot_ref, cot_row_ref, norms_ref, *refs, packed):
    if packed:
        block_refs, refs = refs[:packed], refs[packed:]
        out_ref, out_row_ref, dz_ref, dz_row_ref, e_ref, sums_ref = refs[:6]
        grad_refs, refs = refs[6 : 6 + packed], refs[6 + packed :]
        dz_s, gup_s, gdown_s, acc_s, h_s, dg_s, g_s, eh_s, up_ref, down_ref = refs
    else:
        up_ref, down_ref, out_ref, out_row_ref, dz_ref, dz_row_ref, e_ref, sums_ref = refs[:8]
        grad_refs, refs = refs[8:10], refs[10:]
        dz_s, gup_s, gdown_s, acc_s, h_s, dg_s, g_s, eh_s = refs
    rows, width = z_ref.shape
    hidden = up_ref.shape[1]
    step = pl.program_id(0)

    @pl.when(step == 0)
    def _():
        if packed:
            assemble_mlp(place_ref, block_refs, up_ref, down_ref)
        dz_s[...] = jnp.zeros_like(dz_s)
        gup_s[...] = jnp.zeros_like(gup_s)
        gdown_s[...] = jnp.zeros_like(gdown_s)
        sums_ref[...] = jnp.zeros_like(sums_ref)

    build_windows(dz_s, cot_ref, cot_row_ref)
    hat, inv_std = normalise(z_ref[...])
    u = (hat * norms_ref[2:3] + norms_ref[5:6]).astype(BF16)
    e2 = dz_s[...].astype(BF16)
    ones = jnp.ones((16, rows), BF16)
    ut = jnp.concatenate([u.T, ones], axis=0)
    et = e2.T
    chunks = hidden // width
    strip = 16
    half = width // 2

    def begin(c):
        def up(n):
            cols = slice(c * width + n, c * width + n + half)
            h_s[c % 2, :, n : n + half] = dot_nn(u, up_ref[:, cols])

        def down(n):
            cols = slice(c * width + n, c * width + n + half)
            dg_s[c % 2, :, n : n + half] = dot_nt(e2, down_ref[cols, :])

        return [partial(f, n) for n in (0, half) for f in (up, down)]

    def middle(c):
        def part(r):
            bias = norms_ref[9 + c : 10 + c]
            g, slope = gelu_pair(h_s[c % 2, r : r + strip] + bias)
            g_s[c % 2, r : r + strip] = g.astype(BF16)
            eh_s[c % 2, r : r + strip] = (dg_s[c % 2, r : r + strip] * slope).astype(BF16)

        return [partial(part, r) for r in range(0, rows, strip)]

    def finish(c):
        whole = slice(c * width, (c + 1) * width)

        def add(ref, i, n, x):
            if c == 0:
                ref[i, :, n : n + half] = x
            else:
                ref[i, :, n : n + half] += x

        def forward(n):
            add(acc_s, 0, n, dot_nn(g_s[c % 2], down_ref[whole, n : n + half]))

        def back(n):
            add(acc_s, 1, n, dot_nt(eh_s[c % 2], up_ref[n : n + half, whole]))

        def down(n):
            cols = slice(c * width + n, c * width + n + half)
            gdown_s[:, cols] += dot_nn(et, g_s[c % 2, :, n : n + half])

        def up(n):
            cols = slice(c * width + n, c * width + n + half)
            gup_s[:, cols] += dot_nn(ut, eh_s[c % 2, :, n : n + half])

        return [partial(f, n) for n in (0, half) for f in (forward, back, down, up)]

    for f in begin(0):
        f()
    for c in range(chunks):
        products = begin(c + 1) if c + 1 < chunks else []
        if c > 0:
            products = products + finish(c - 1)
        strips = middle(c)
        done = 0
        for i, f in enumerate(strips):
            f()
            upto = len(products) * (i + 1) // len(strips)
            for g in products[done:upto]:
                g()
            done = upto
    for f in finish(chunks - 1):
        f()
    z2 = z_ref[...] + acc_s[0] + norms_ref[13:14]
    split_windows(z2, out_ref, out_row_ref)
    du = acc_s[1]
    dz2 = dz_s[...]
    sums_ref[1:2, :width] += jnp.sum(e2.astype(F32), axis=0, keepdims=True)
    sums_ref[2:3, :width] += jnp.sum(du * hat, axis=0, keepdims=True)
    sums_ref[3:4, :width] += jnp.sum(du, axis=0, keepdims=True)
    dz1 = dz2 + norm_back(du, hat, inv_std, norms_ref[2:3])
    dz_ref[...] = dz1
    local_len = cot_ref.shape[1]
    for w in range(cot_ref.shape[0]):
        at = w * PITCH + local_len
        dz_row_ref[w : w + 1] = dz1[at : at + 1]
    e = dz1.astype(BF16)
    e_ref[...] = e
    sums_ref[4:5, :width] += jnp.sum(e.astype(F32), axis=0, keepdims=True)

    @pl.when(step == pl.num_programs(0) - 1)
    def _():
        sums_ref[0:1, :] = gup_s[width : width + 1, :]
        if packed:
            pack_mlp(place_ref, gup_s, gdown_s, grad_refs)
        else:
            grad_refs[0][...] = gup_s[:width].astype(BF16)
            grad_refs[1][...] = gdown_s[...].astype(BF16)


def window_backward_kernel(
    e_ref,
    qkv_ref,
    p_ref,
    hat_ref,
    o_ref,
    wproj_ref,
    *refs,
    local_len,
):
    mixed_ref, mixed_row_ref, sums_ref, gqkv_ref, gproj_ref, do_s, mixed_s = refs[1:]
    rows, width = e_ref.shape
    count = qkv_ref.shape[0]

    @pl.when(pl.program_id(0) == 0)
    def _():
        do_s[rows:, :] = jnp.zeros((do_s.shape[0] - rows, width), F32)
        for ref in (sums_ref, gqkv_ref, gproj_ref):
            ref[...] = jnp.zeros_like(ref)

    do_s[:rows, :] = dot_nt(e_ref[...], wproj_ref[...])
    gproj_ref[...] += dot_tn(o_ref[...], e_ref[...])
    masks = head_masks(SLOT)

    spots = [c * LANES for c in range(width // LANES)]

    def window(w):
        base = pl.multiple_of(w * PITCH, 8)
        upstream, slopes = [], []
        for at in spots:
            do = spread(do_s[pl.ds(base, SLOT), at : at + LANES].astype(BF16), masks)
            v = qkv_ref[w, :, 2 * width + at : 2 * width + at + LANES]
            slopes.append(dot_nt(v, do))
            upstream.append(do)
        for c, at in enumerate(spots):
            dv = dot_nn(p_ref[w, c], upstream[c])
            mixed_s[pl.ds(base, PITCH), 2 * width + at : 2 * width + at + LANES] = dv[:PITCH]
        scores = []
        for c, dp in enumerate(slopes):
            p = p_ref[w, c].astype(F32)
            ds = p * (dp - jnp.sum(dp * p, axis=0, keepdims=True))
            scores.append(ds.astype(BF16))
        turned = [turn(ds) for ds in scores]
        for at, ds in zip(spots, scores):
            dk = dot_nn(ds, spread(qkv_ref[w, :, at : at + LANES], masks)) * FACTOR
            mixed_s[pl.ds(base, PITCH), width + at : width + at + LANES] = dk[:PITCH]
        for at, ds in zip(spots, turned):
            k = qkv_ref[w, :, width + at : width + at + LANES]
            dq = dot_nn(ds, spread(k, masks, TURNED)) * FACTOR
            mixed_s[pl.ds(base, PITCH), at : at + LANES] = dq[:PITCH]

    def windows(i, carry):
        for j in range(2):
            window(2 * i + j)
        return carry

    lax.fori_loop(0, count // 2, windows, 0)
    mixed = mixed_s[...].astype(BF16)
    mixed_ref[...] = mixed
    for w in range(count):
        at = w * PITCH + local_len
        mixed_row_ref[w : w + 1] = mixed_s[at : at + 1].astype(BF16)
    sums_ref[0:1, :] += jnp.sum(mixed.astype(F32), axis=0, keepdims=True)
    gqkv_ref[...] += dot_tn(hat_ref[...], mixed)


def local_back_kernel(local_ref, dz_ref, mixed_ref, wqkv_ref, norms_ref, *refs):
    out_ref, tick_ref, z_s = refs[-3:]
    tick_ref[...] = jnp.zeros_like(tick_ref)
    count, local_len, _ = local_ref.shape

    @pl.when(pl.program_id(0) == 0)
    def _():
        z_s[...] = jnp.zeros_like(z_s)

    for w in range(count):
        z_s[w * PITCH : w * PITCH + local_len] = local_ref[w].astype(F32)
    du = dot_nt(mixed_ref[...], wqkv_ref[...])
    hat, inv_std = normalise(z_s[...])
    dz0 = dz_ref[...] + norm_back(du, hat, inv_std, norms_ref[1:2])
    for w in range(count):
        out_ref[w] = dz0[w * PITCH : w * PITCH + local_len].astype(BF16)


def pack_attention(place_ref, gqkv_s, gproj_s, small_s, du_s, own, outs):
    wide, deep = outs[0].shape[:2]
    peers = wide * deep
    width = gproj_s.shape[0]
    rows = width // peers
    quads = width // LANES
    counts = [gqkv_s.shape[1] // len(outs) // LANES, gproj_s.shape[1] // len(outs) // LANES]
    far, me = place_ref[0], place_ref[1]
    linear = far * peers + me
    near = du_s.shape[0] // own
    for r, out in enumerate(outs):
        d = r ^ far
        for p in range(peers):
            j, i = p % wide, p // wide
            f = me ^ p
            here = pl.ds(pl.multiple_of(f * rows, 8), rows)
            row = 0
            for count, grad in zip(counts, (gqkv_s, gproj_s)):
                for c in range(count):
                    at = pl.ds(pl.multiple_of((d * count + c) * LANES, LANES), LANES)
                    out[j, i, row : row + rows] = grad[here, at].astype(BF16)
                    row += rows
            out[j, i, row : row + rows] = small_s[here].astype(BF16)
            row += rows
            away = d * peers + f - linear + near // 2
            inside = (away >= 0) & (away < near)
            at = pl.ds(pl.multiple_of(jnp.where(inside, away, 0) * own, 8), own)
            share = jnp.where(inside, 1.0, 0.0)
            for c in range(quads):
                term = du_s[at, c * LANES : (c + 1) * LANES] * share
                out[j, i, row : row + own] = term.astype(BF16)
                row += own


def region_tail_kernel(
    place_ref,
    mixed_row_ref,
    dz_row_ref,
    mid_ref,
    hat_ref,
    qkv_ref,
    p_ref,
    o_ref,
    wqkv_ref,
    wproj_ref,
    norms_ref,
    gqkv_in_ref,
    gproj_in_ref,
    att_sums_ref,
    mlp_sums_ref,
    dmid_ref,
    *refs,
    packed,
):
    outs, refs = (refs[:packed], refs[packed:]) if packed else (refs[:4], refs[4:])
    near_s, du_s, gqkv_s, gproj_s, lines_s, small_s = refs
    own, width = mid_ref.shape
    rows = qkv_ref.shape[0]
    first = (rows - own) // 2
    mine = slice(first, first + own)

    mid_hat, mid_std = normalise(mid_ref[...])
    row_du = dot_nt(mixed_row_ref[...], wqkv_ref[...])
    dmid = dz_row_ref[...] + norm_back(row_du, mid_hat, mid_std, norms_ref[1:2])
    dmid_ref[...] = dmid
    e = dmid.astype(BF16)
    do = dot_nt(e, wproj_ref[...])
    do = jnp.concatenate([do, jnp.zeros((SLOT - own, width), F32)], axis=0).astype(BF16)
    masks = head_masks(SLOT)
    out_masks = [m.astype(F32) for m in masks]
    dqs = []
    for c in range(width // LANES):
        at = c * LANES
        q = qkv_ref[first : first + SLOT, at : at + LANES]
        k = qkv_ref[:, width + at : width + at + LANES]
        v = qkv_ref[:, 2 * width + at : 2 * width + at + LANES]
        dox = spread(do[:, at : at + LANES], masks)
        p = p_ref[c]
        near_s[:, width + at : width + at + LANES] = dot_nn(p, dox).astype(BF16)
        dp = dot_nt(v, dox)
        pf = p.astype(F32)
        ds = (pf * (dp - jnp.sum(dp * pf, axis=0, keepdims=True))).astype(BF16)
        near_s[:, at : at + LANES] = (dot_nn(ds, spread(q, masks)) * FACTOR).astype(BF16)
        wide = dot_tn(ds, k)
        dq = sum(wide[h * SLOT : (h + 1) * SLOT] * out_masks[h] for h in range(GROUP))
        dqs.append((dq[:own] * FACTOR).astype(BF16))
    dq = jnp.concatenate(dqs, axis=1)
    near = near_s[...]

    du_s[...] = dot_nt(near, wqkv_ref[:, width:])
    du_s[mine] += dot_nt(dq, wqkv_ref[:, :width])

    win_sum = att_sums_ref[0:1]
    near_sum = jnp.concatenate(
        [
            jnp.sum(dq.astype(F32), axis=0, keepdims=True),
            jnp.sum(near.astype(F32), axis=0, keepdims=True),
        ],
        axis=1,
    )
    sums = jnp.concatenate([near_sum, win_sum, jnp.zeros((6, 3 * width), F32)], axis=0)
    high = sums.astype(BF16)
    rest = (sums - high.astype(F32)).astype(BF16)
    both = jnp.concatenate([high, rest], axis=0)
    shifts = dot_nt(both, wqkv_ref[...])
    shifts = shifts[:8] + shifts[8:]
    lines_s[...] = jnp.zeros_like(lines_s)
    lines_s[:16] = norms_ref[...]
    columns = lines_s[...].T
    gain_0, gain_1 = columns[:, 0:1], columns[:, 1:2]
    shift_0, shift_1 = columns[:, 3:4], columns[:, 4:5]
    dgain_0 = jnp.zeros((width, 1), F32)
    dgain_1 = jnp.zeros((width, 1), F32)
    for i in range(3):
        cols = slice(i * width, (i + 1) * width)
        if i == 0:
            region = dot_tn(hat_ref[mine, :], dq)
        else:
            region = dot_tn(hat_ref[...], near[:, (i - 1) * width : i * width])
        window = gqkv_in_ref[:, cols]
        weight = wqkv_ref[:, cols].astype(F32)
        dgain_0 += jnp.sum(weight * region, axis=1, keepdims=True)
        dgain_1 += jnp.sum(weight * window, axis=1, keepdims=True)
        gqkv_s[:, cols] = (
            region * gain_0
            + window * gain_1
            + shift_0 * near_sum[:, cols]
            + shift_1 * win_sum[:, cols]
        )
    gproj_s[...] = gproj_in_ref[...] + dot_tn(o_ref[...], e)
    total = near_sum + win_sum
    hidden = mlp_sums_ref.shape[1]
    lines = [
        None,
        None,
        mlp_sums_ref[2:3, :width],
        shifts[0:1],
        shifts[1:2],
        mlp_sums_ref[3:4, :width],
        total[:, :width],
        total[:, 2 * width :],
        jnp.sum(e.astype(F32), axis=0, keepdims=True) + mlp_sums_ref[4:5, :width],
    ]
    lines += [mlp_sums_ref[0:1, c * width : (c + 1) * width] for c in range(hidden // width)]
    lines += [mlp_sums_ref[1:2, :width]]
    lines_s[...] = jnp.zeros_like(lines_s)
    for i, line in enumerate(lines):
        if line is not None:
            lines_s[i : i + 1] = line
    small_s[...] = lines_s[...].T
    small_s[:, 0:1] = dgain_0
    small_s[:, 1:2] = dgain_1
    if packed:
        pack_attention(place_ref, gqkv_s, gproj_s, small_s, du_s, own, outs)
    else:
        outs[0][...] = gqkv_s[...].astype(BF16)
        outs[1][...] = gproj_s[...].astype(BF16)
        outs[2][...] = small_s[...]
        outs[3][...] = du_s[...].astype(BF16)


def finish_kernel(
    x_ref,
    dmid_ref,
    norms_ref,
    mlp_ref,
    *refs,
    terms,
):
    term_refs, outs = refs[:terms], refs[terms + 1 : -1]
    out_ref, gqkv_ref, gproj_ref, gup_ref, gdown_ref, ggains_ref, gbiases_ref = outs
    small_s = refs[-1]
    own, width = x_ref.shape

    def total(row, count):
        here = slice(row, row + count)
        return sum([t[here].astype(F32) for t in term_refs[1:]], term_refs[0][here].astype(F32))

    rows = gqkv_ref.shape[0]
    row = 0
    for ref in (gqkv_ref, gproj_ref):
        for c in range(0, ref.shape[1], LANES):
            ref[:, c : c + LANES] = total(row, rows)
            row += rows
    small_s[:rows] = total(row, rows)
    small = small_s[...].T
    count = ggains_ref.shape[0]
    ggains_ref[...] = small[:count, :rows]
    gbiases_ref[...] = small[count : count + gbiases_ref.shape[0], :rows]
    row += rows
    du = jnp.concatenate([total(row + c * own, own) for c in range(width // LANES)], axis=1)
    hat, inv_std = normalise(x_ref[...].astype(F32))
    out_ref[...] = (dmid_ref[...] + norm_back(du, hat, inv_std, norms_ref[0:1])).astype(BF16)
    row = 0
    for c in range(0, gup_ref.shape[1], LANES):
        gup_ref[:, c : c + LANES] = mlp_ref[row : row + rows].astype(F32)
        row += rows
    gdown_ref[...] = mlp_ref[row:].astype(F32).T


def region_end_kernel(x_ref, dmid_ref, norms_ref, *refs):
    near_refs, out_ref = refs[:-1], refs[-1]
    du = near_refs[0][...].astype(F32)
    for ref in near_refs[1:]:
        du = du + ref[...].astype(F32)
    hat, inv_std = normalise(x_ref[...].astype(F32))
    out_ref[...] = (dmid_ref[...] + norm_back(du, hat, inv_std, norms_ref[0:1])).astype(BF16)


def axis_rounds(size):
    rounds = []
    shift = 0
    while (1 << shift) < size:
        width = min(4, size >> shift)
        rounds.append((shift, width))
        shift += width.bit_length() - 1
    return rounds


def swap_by(x, axis, code):
    pairs = [(i, i ^ code) for i in range(lax.axis_size(axis))]
    return lax.ppermute(x, axis, pairs)


def gather_axis(x, axis, stacked=True):
    size = lax.axis_size(axis)
    rounds = axis_rounds(size)
    if not stacked and len(rounds) == 1:
        return [x] + [swap_by(x, axis, j) for j in range(1, size)], list(range(size))
    stack = x[None]
    codes = [0]
    for shift, width in reversed(rounds):
        parts = [stack] + [swap_by(stack, axis, j << shift) for j in range(1, width)]
        stack = jnp.concatenate(parts, axis=0)
        codes = [c ^ (j << shift) for j in range(width) for c in codes]
    return stack, codes


def in_order(stack, codes, axis):
    place = [0] * len(codes)
    for p, c in enumerate(codes):
        place[c] = p
    wanted = jnp.arange(len(codes), dtype=jnp.int32) ^ lax.axis_index(axis)
    return jnp.take(stack, jnp.asarray(place, dtype=jnp.int32)[wanted], axis=0)


def scatter_axis(blocks, axis):
    size = lax.axis_size(axis)
    me = lax.axis_index(axis)
    rest = blocks.shape[1:]
    for shift, width in axis_rounds(size):
        left = blocks.shape[0] // width
        cut = blocks.reshape((left, width) + rest)
        mine = (me >> shift) & (width - 1)
        total = lax.dynamic_index_in_dim(cut, mine, 1, keepdims=False).astype(jnp.float32)
        for j in range(1, width):
            out = lax.dynamic_index_in_dim(cut, mine ^ j, 1, keepdims=False)
            total = total + swap_by(out, axis, j << shift).astype(jnp.float32)
        blocks = total.astype(blocks.dtype)
    return blocks[0]


def join(blocks):
    dp, fsdp, rows, cols = blocks.shape
    return blocks.transpose(1, 2, 0, 3).reshape(fsdp * rows, dp * cols)


def cut(whole, dp, fsdp):
    rows, cols = whole.shape
    return whole.reshape(fsdp, rows // fsdp, dp, cols // dp).transpose(2, 0, 1, 3)


def scatter_all(blocks):
    return scatter_axis(scatter_axis(blocks, "dp"), "fsdp").astype(jnp.float32)


def shifted(x, by):
    axes = ("dp", "fsdp")
    peers = lax.axis_size(axes)
    pairs = [(i, i + by) for i in range(peers) if 0 <= i + by < peers]
    return lax.ppermute(x, axes, pairs)


def matched(x, by, second):
    axes = ("dp", "fsdp")
    peers = lax.axis_size(axes)
    pairs = []
    for i in range(peers):
        low = i % (2 * by) < by
        to = i + by if low != bool(second) else i - by
        if 0 <= to < peers:
            pairs.append((i, to))
    return lax.ppermute(x, axes, pairs)


def full(shape):
    return pl.BlockSpec(shape, lambda *_: (0,) * len(shape))


def tiled(shape, begin=0):
    return pl.BlockSpec(shape, lambda i: (i + begin,) + (0,) * (len(shape) - 1))


def like(shape, dtype):
    return jax.ShapeDtypeStruct(shape, dtype)


def smem():
    return pl.BlockSpec(memory_space=pltpu.SMEM)


def vmem():
    return pl.BlockSpec(memory_space=pltpu.VMEM)


def gather_round(stack, axis, which):
    shift, width = axis_rounds(lax.axis_size(axis))[::-1][which]
    return [stack] + [swap_by(stack, axis, j << shift) for j in range(1, width)]


def gather_parts(block, axis):
    rounds = axis_rounds(lax.axis_size(axis))[::-1]
    parts = [block[None]]
    codes = [0]
    for which, (shift, width) in enumerate(rounds):
        parts = gather_round(jnp.concatenate(parts, axis=0), axis, which)
        codes = [c ^ (j << shift) for j in range(width) for c in codes]
    return parts, codes


def far_parts(parts):
    return parts + [
        swap_by(x, "dp", r) for r in range(1, lax.axis_size("dp")) for x in parts
    ]


def send_far(grads):
    return [swap_by(g, "dp", r) for r, g in enumerate(grads) if r > 0]


def send_round(terms, step):
    return [swap_by(x, "fsdp", j * step) for j, x in enumerate(terms) if j > 0]


def reduce_round(terms, got):
    total = terms[0].astype(F32)
    for x in got:
        total = total + x.astype(F32)
    return total.astype(BF16)


def takes(us):
    return pl.CostEstimate(flops=int(us * 1.1e9), bytes_accessed=int(us * 1e6), transcendentals=0)


def params():
    return pltpu.CompilerParams(vmem_limit_bytes=VMEM_BYTES)


def on_device(
    x_regional,
    x_local,
    w_qkv,
    w_proj,
    w_fc1,
    w_fc2,
    gains,
    biases,
    region_counts,
    cot_regional,
    cot_local,
):
    regions, local_len, width = x_local.shape
    group = 8
    steps = regions // group
    rows = group * PITCH
    all_rows = regions * PITCH
    quads = width // LANES
    span = (regions + MAX_REGIONS - 2) // regions
    all_regions = regions * lax.axis_size(("dp", "fsdp"))
    linear = lax.axis_index(("dp", "fsdp"))
    first_row = linear * regions
    dp, fsdp = lax.axis_size("dp"), lax.axis_size("fsdp")
    qkv_cols, proj_cols = w_qkv.shape[1], w_proj.shape[1]
    in_blocks = qkv_cols % LANES == 0 and proj_cols % LANES == 0 and w_fc2.shape[0] == LANES
    small_rows = gains.shape[0] + biases.shape[0]

    mlp_cols = w_fc2.shape[1]
    if in_blocks:
        att_rows = (qkv_cols + proj_cols + LANES) // LANES * w_qkv.shape[0]
        mlp_rows = w_fc1.shape[0] * w_fc1.shape[1] // mlp_cols + w_fc2.shape[0]
        att_block, mlp_block = pl.pallas_call(
            pack_weights_kernel,
            out_shape=(like((att_rows, LANES), BF16), like((mlp_rows, mlp_cols), BF16)),
            scratch_shapes=[pltpu.VMEM((LANES, LANES), F32)],
            compiler_params=params(),
            cost_estimate=takes(2),
            name="pack_weights",
        )(w_qkv, w_proj, gains, biases, w_fc1, w_fc2)
    else:
        small = jnp.concatenate([gains, biases], axis=0).T
        small = jnp.pad(small, ((0, 0), (0, LANES - small_rows)))
        att_block = jnp.concatenate([w_qkv, w_proj, small], axis=1)
        up_parts = [w_fc1[:, i : i + mlp_cols] for i in range(0, w_fc1.shape[1], mlp_cols)]
        mlp_block = jnp.concatenate(up_parts + [w_fc2], axis=0)
    hidden = w_fc1.shape[1] * dp

    place = jnp.stack([lax.axis_index("dp"), lax.axis_index("fsdp")]).astype(jnp.int32)
    near_rows = (2 * span + 1) * regions
    wide = axis_rounds(fsdp)[0][1]
    if in_blocks:
        att_parts, order = gather_parts(att_block, "fsdp")
        codes = (order, dp)
        att_stacks = far_parts(att_parts)
        near = [x_regional]
        near += [matched(x_regional, d, s) for d in range(1, span + 1) for s in range(2)]
        mlp_half = lax.all_gather(mlp_block, "fsdp", axis=0, tiled=False)
    else:
        att_stack, order = gather_axis(att_block, "fsdp")
        codes = (order, dp)
        att_stacks, far_codes = gather_axis(att_stack, "dp")
        mlp_stack, _ = gather_axis(mlp_block, "fsdp")
        mlp_stack = in_order(mlp_stack, order, "fsdp")
        mlp_stack, _ = gather_axis(mlp_stack, "dp")
        mlp_stack = in_order(mlp_stack, far_codes, "dp")

    image_ends = jnp.minimum(jnp.cumsum(region_counts), all_regions)
    key_rows = first_row - span * regions + jnp.arange(near_rows, dtype=jnp.int32)
    key_image = jnp.sum((image_ends[None, :] <= key_rows[:, None]).astype(jnp.int32), axis=1)
    inside = (key_rows >= 0) & (key_rows < all_regions)
    key_image = jnp.where(inside, key_image, -1)
    query_image = jnp.pad(
        key_image[span * regions : (span + 1) * regions],
        (0, SLOT - regions),
        constant_values=-2,
    )
    query_image = jnp.tile(query_image, GROUP)[None]

    region_outs = (
        like((regions, width), F32),
        like((near_rows, width), BF16),
        like((near_rows, 3 * width), BF16),
        like((quads, near_rows, GROUP * SLOT), BF16),
        like((regions, width), BF16),
    )
    if in_blocks:
        whole = (
            like((width, 3 * width), BF16),
            like((width, width), BF16),
            like((16, width), F32),
        )
        region_mid, region_hat, region_qkv, region_p, region_o, qkv_full, proj_full, norms = (
            pl.pallas_call(
                partial(
                    region_forward_kernel, near=len(near), stacks=len(att_stacks), codes=codes
                ),
                in_specs=[smem()] + [vmem()] * (2 + len(near) + len(att_stacks)),
                out_shape=region_outs + whole,
                scratch_shapes=[
                    pltpu.VMEM((width, LANES), F32),
                    pltpu.VMEM((near_rows, width), F32),
                ],
                compiler_params=params(),
                cost_estimate=takes(6),
                name="region_forward",
            )(place, key_image[:, None], query_image, *near, *att_stacks)
        )
    else:
        near = [
            x_regional if offset == 0 else shifted(x_regional, -offset)
            for offset in range(-span, span + 1)
        ]
        blocks = in_order(jnp.stack([in_order(s, order, "fsdp") for s in att_stacks]), far_codes, "dp")
        qkv_full = join(blocks[..., :qkv_cols])
        proj_full = join(blocks[..., qkv_cols : qkv_cols + proj_cols])
        small = blocks[0, :, :, qkv_cols + proj_cols :].reshape(width, LANES)
        norms = small.astype(F32).T[:16]
        region_mid, region_hat, region_qkv, region_p, region_o = pl.pallas_call(
            partial(region_forward_kernel, near=len(near), stacks=0, codes=codes),
            in_specs=[smem()] + [vmem()] * (5 + len(near)),
            out_shape=region_outs,
            compiler_params=params(),
            cost_estimate=takes(6),
            name="region_forward",
        )(place, key_image[:, None], query_image, *near, qkv_full, proj_full, norms)

    first_half = steps // 2
    forward_outs = (
        like((all_rows, width), F32),
        like((all_rows, width), BF16),
        like((regions, SLOT, 3 * width), BF16),
        like((regions, quads, SLOT, GROUP * SLOT), BF16),
        like((all_rows, width), BF16),
        like((8, LANES), F32),
    )

    def window_forward(begin, count, held, ties):
        operands = (x_local, region_mid, qkv_full, proj_full, norms)
        return pl.pallas_call(
            window_forward_kernel,
            grid=(count,),
            in_specs=[
                tiled((group, local_len, width), begin),
                tiled((group, width), begin),
                full(qkv_full.shape),
                full(proj_full.shape),
                full(norms.shape),
            ]
            + [pl.BlockSpec(memory_space=pl.ANY)] * (len(held) + len(ties)),
            out_specs=[
                tiled((rows, width), begin),
                tiled((rows, width), begin),
                tiled((group, SLOT, 3 * width), begin),
                tiled((group, quads, SLOT, GROUP * SLOT), begin),
                tiled((rows, width), begin),
                full((8, LANES)),
            ],
            out_shape=forward_outs,
            scratch_shapes=[
                pltpu.VMEM((rows, width), F32),
                pltpu.VMEM((rows + 8, 3 * width), F32),
                pltpu.VMEM((rows, width), F32),
            ],
            input_output_aliases={len(operands) + i: i for i in range(len(held))},
            compiler_params=params(),
            cost_estimate=takes(6 * count),
            name="window_forward",
        )(*operands, *held, *ties)

    *held, tick = window_forward(0, first_half, (), ())
    if in_blocks:
        mlp_half, tick = lax.optimization_barrier((mlp_half, tick))
        mlp_stacks = far_parts([mlp_half])
    z1, win_hat, win_qkv, win_p, win_o, _ = window_forward(
        first_half, steps - first_half, held, (tick,)
    )

    mlp_outs = [
        like(x_local.shape, BF16),
        like(x_regional.shape, BF16),
        like((all_rows, width), F32),
        like(x_regional.shape, F32),
        like((all_rows, width), BF16),
        like((8, hidden), F32),
    ]
    mlp_specs = [
        tiled((group, local_len, width)),
        tiled((group, width)),
        tiled((rows, width)),
        tiled((group, width)),
        tiled((rows, width)),
        full((8, hidden)),
    ]
    mlp_scratch = [
        pltpu.VMEM((rows, width), F32),
        pltpu.VMEM((width + 16, hidden), F32),
        pltpu.VMEM((width, hidden), F32),
        pltpu.VMEM((2, rows, width), F32),
        pltpu.VMEM((2, rows, width), F32),
        pltpu.VMEM((2, rows, width), F32),
        pltpu.VMEM((2, rows, width), BF16),
        pltpu.VMEM((2, rows, width), BF16),
    ]
    if in_blocks:
        weights = tuple(mlp_stacks)
        tall = mlp_block.shape[0] * mlp_cols // LANES
        grad_shapes = [(fsdp, tall, LANES)] * dp
        mlp_scratch += [pltpu.VMEM((width, hidden), BF16), pltpu.VMEM((hidden, width), BF16)]
    else:
        blocks = mlp_stack.transpose(1, 0, 2, 3)
        up_full = blocks[:, :, : mlp_block.shape[0] - w_fc2.shape[0]]
        up_full = up_full.reshape(fsdp, dp, -1, w_fc1.shape[0], mlp_cols)
        up_full = up_full.transpose(0, 3, 1, 2, 4).reshape(width, hidden)
        down_full = blocks[:, :, mlp_block.shape[0] - w_fc2.shape[0] :]
        down_full = down_full.transpose(0, 2, 1, 3).reshape(hidden, width)
        weights = (up_full, down_full)
        grad_shapes = [(width, hidden)] * 2
    out_local, out_regional, dz1, dz_row, win_e, mlp_sums, *mlp_grads = pl.pallas_call(
        partial(mlp_kernel, packed=dp if in_blocks else 0),
        grid=(steps,),
        in_specs=[
            smem(),
            tiled((rows, width)),
            tiled((group, local_len, width)),
            tiled((group, width)),
            full(norms.shape),
        ]
        + [full(w.shape) for w in weights],
        out_specs=mlp_specs + [full(g) for g in grad_shapes],
        out_shape=mlp_outs + [like(g, BF16) for g in grad_shapes],
        scratch_shapes=mlp_scratch,
        compiler_params=params(),
        cost_estimate=takes(50),
        name="mlp",
    )(place, z1, cot_local, cot_regional, norms, *weights)

    if in_blocks:
        mlp_sum = mlp_grads[0].astype(F32)
        for g in send_far(mlp_grads):
            mlp_sum = mlp_sum + g.astype(F32)
        mlp_chip = mlp_sum.astype(BF16)
        mlp_sum = lax.psum_scatter(mlp_chip, "fsdp", scatter_dimension=0)

    win_mixed, mixed_row, att_sums, grad_qkv, grad_proj = pl.pallas_call(
        partial(window_backward_kernel, local_len=local_len),
        grid=(steps,),
        in_specs=[
            tiled((rows, width)),
            tiled((group, SLOT, 3 * width)),
            tiled((group, quads, SLOT, GROUP * SLOT)),
            tiled((rows, width)),
            tiled((rows, width)),
            full(proj_full.shape),
            pl.BlockSpec(memory_space=pl.ANY),
        ],
        out_specs=[
            tiled((rows, 3 * width)),
            tiled((group, 3 * width)),
            full((8, 3 * width)),
            full((width, 3 * width)),
            full((width, width)),
        ],
        out_shape=(
            like((all_rows, 3 * width), BF16),
            like((regions, 3 * width), BF16),
            like((8, 3 * width), F32),
            like((width, 3 * width), F32),
            like((width, width), F32),
        ),
        scratch_shapes=[
            pltpu.VMEM((rows + 8, width), F32),
            pltpu.VMEM((rows, 3 * width), F32),
        ],
        compiler_params=params(),
        name="window_backward",
    )(win_e, win_qkv, win_p, win_hat, win_o, proj_full, mlp_chip if in_blocks else norms)

    if in_blocks:
        tall = att_rows + regions * quads
        grad_shapes = [like((wide, fsdp // wide, tall, LANES), BF16)] * dp
    else:
        grad_shapes = [
            like((width, 3 * width), BF16),
            like((width, width), BF16),
            like((width, LANES), F32),
            like((near_rows, width), BF16),
        ]
    operands = (
        mixed_row,
        dz_row,
        region_mid,
        region_hat,
        region_qkv,
        region_p,
        region_o,
        qkv_full,
        proj_full,
        norms,
        grad_qkv,
        grad_proj,
        att_sums,
        mlp_sums,
    )
    dmid, *att_grads = pl.pallas_call(
        partial(region_tail_kernel, packed=dp if in_blocks else 0),
        in_specs=[smem()] + [vmem()] * len(operands),
        out_shape=[like((regions, width), F32)] + grad_shapes,
        scratch_shapes=[
            pltpu.VMEM((near_rows, 2 * width), BF16),
            pltpu.VMEM((near_rows, width), F32),
            pltpu.VMEM((width, 3 * width), F32),
            pltpu.VMEM((width, width), F32),
            pltpu.VMEM((LANES, width), F32),
            pltpu.VMEM((width, LANES), F32),
        ],
        compiler_params=params(),
        name="region_tail",
    )(place, *operands)

    def local_back(begin, count, ties, held):
        return pl.pallas_call(
            local_back_kernel,
            grid=(count,),
            in_specs=[
                tiled((group, local_len, width), begin),
                tiled((rows, width), begin),
                tiled((rows, 3 * width), begin),
                full(qkv_full.shape),
                full(norms.shape),
            ]
            + [pl.BlockSpec(memory_space=pl.ANY)] * (len(ties) + len(held)),
            out_specs=[tiled((group, local_len, width), begin), full((8, LANES))],
            out_shape=(like(x_local.shape, BF16), like((8, LANES), F32)),
            scratch_shapes=[pltpu.VMEM((rows, width), F32)],
            input_output_aliases={5: 0} if held else {},
            compiler_params=params(),
            cost_estimate=takes(3 * count),
            name="local_back",
        )(x_local, dz1, win_mixed, qkv_full, norms, *held, *ties)

    cuts = [steps * i // 3 for i in range(4)]

    def local_part(i, ties, held):
        return local_back(cuts[i], cuts[i + 1] - cuts[i], ties, held)

    if in_blocks:
        far = send_far(att_grads)
        grad_local, tick = local_part(0, (att_grads[0],), ())
        (*far, tick) = lax.optimization_barrier((*far, tick))
        terms = [
            sum([g[j].astype(F32) for g in far], att_grads[0][j].astype(F32)).astype(BF16)
            for j in range(wide)
        ]
        got = send_round(terms, 1)
        grad_local, tick = local_part(1, (tick, terms[0]), (grad_local,))
        grad_local, tick = local_part(2, (), (grad_local,))
        (*got, tick) = lax.optimization_barrier((*got, tick))
        terms = reduce_round(terms, got)
        terms = [terms[j] for j in range(fsdp // wide)]
        terms = terms[:1] + send_round(terms, wide)
        operands = (x_regional, dmid, norms, mlp_sum, *terms, tick)
        out_specs = (
            like(x_regional.shape, BF16),
            like(w_qkv.shape, F32),
            like(w_proj.shape, F32),
            like(w_fc1.shape, F32),
            like(w_fc2.shape, F32),
            like(gains.shape, F32),
            like(biases.shape, F32),
        )
        grad_regional, grad_qkv, grad_proj, grad_up, grad_down, grad_gains, grad_biases = (
            pl.pallas_call(
                partial(finish_kernel, terms=len(terms)),
                in_specs=[vmem()] * (len(operands) - 1) + [pl.BlockSpec(memory_space=pl.ANY)],
                out_shape=out_specs,
                scratch_shapes=[pltpu.VMEM((LANES, LANES), F32)],
                compiler_params=params(),
                cost_estimate=takes(2),
                name="finish",
            )(*operands)
        )
    else:
        up_rows = w_fc1.shape[0]
        up_blocks = cut(mlp_grads[0], dp, fsdp).reshape(dp, fsdp, up_rows, -1, mlp_cols)
        up_blocks = up_blocks.transpose(0, 1, 3, 2, 4).reshape(dp, fsdp, -1, mlp_cols)
        down_blocks = cut(mlp_grads[1].T, dp, fsdp)
        mlp_sum = scatter_all(jnp.concatenate([up_blocks, down_blocks], axis=2))
        grad_up = mlp_sum[: up_blocks.shape[2]].reshape(-1, up_rows, mlp_cols)
        grad_up = grad_up.transpose(1, 0, 2).reshape(w_fc1.shape)
        grad_down = mlp_sum[up_blocks.shape[2] :]
        grad_qkv, grad_proj, small, du_near = att_grads
        small = small.astype(BF16).reshape(1, fsdp, -1, LANES)
        small = jnp.broadcast_to(small, (dp,) + small.shape[1:])
        blocks = [cut(grad_qkv, dp, fsdp), cut(grad_proj, dp, fsdp), small]
        att = scatter_all(jnp.concatenate(blocks, axis=3))
        grad_qkv = att[:, :qkv_cols]
        grad_proj = att[:, qkv_cols : qkv_cols + proj_cols]
        small = att[:, qkv_cols + proj_cols :].T[:small_rows]
        grad_gains, grad_biases = small[: gains.shape[0]], small[gains.shape[0] :]
        held = ()
        for i in range(3):
            grad_local, tick = local_part(i, (), held)
            held = (grad_local,)
        returned = []
        for offset in range(-span, span + 1):
            part = du_near[(offset + span) * regions : (offset + span + 1) * regions]
            returned.append(part if offset == 0 else shifted(part, offset))
        grad_regional = pl.pallas_call(
            region_end_kernel,
            out_shape=like(x_regional.shape, BF16),
            compiler_params=params(),
            name="region_end",
        )(x_regional, dmid, norms, *returned)
    return (
        out_regional,
        out_local,
        grad_regional,
        grad_local,
        grad_qkv,
        grad_proj,
        grad_up,
        grad_down,
        grad_gains,
        grad_biases,
    )


def solution(mesh):
    in_specs = (
        P(("dp", "fsdp"), None),
        P(("dp", "fsdp"), None, None),
        P("fsdp", "dp"),
        P("fsdp", "dp"),
        P("fsdp", "dp"),
        P("fsdp", "dp"),
        P(None, "fsdp"),
        P(None, "fsdp"),
        P(),
        P(("dp", "fsdp"), None),
        P(("dp", "fsdp"), None, None),
    )
    out_specs = (
        P(("dp", "fsdp"), None),
        P(("dp", "fsdp"), None, None),
        P(("dp", "fsdp"), None),
        P(("dp", "fsdp"), None, None),
        P("fsdp", "dp"),
        P("fsdp", "dp"),
        P("fsdp", "dp"),
        P("fsdp", "dp"),
        P(None, "fsdp"),
        P(None, "fsdp"),
    )
    return jax.shard_map(
        on_device, mesh=mesh, in_specs=in_specs, out_specs=out_specs, check_vma=False
    )
```

time: 1200 us -> 280 us (0.23)
  waiting for transfers between devices: 452 us -> 46 us
  matrix products: 256 us -> 0 us
  local copies, waits for them, and re-layouts: 230 us -> 13 us
  Pallas kernels: 0 us -> 165 us
  blocking collectives: 138 us -> 0 us
  other arithmetic: 68 us -> 7.95 us
    reduce_scatter x8 -> x1, waiting for transfers between devices: 316 us -> 0.02 us  [on_device(): mlp_sum = lax.psum_scatter(mlp_chip, 'fsdp', scatter_dimension=0)]
    dot_general x30 -> x0, matrix products: 256 us -> none  [the longest x1 52.3 us: on_device(): jnp.dot(low_two, up_full, preferred_element_type=jnp.float32) + bias_up]
    pallas_call x0 -> x11, Pallas kernels: none -> 165 us  [the longest x1 56.3 us: on_device(): pl.pallas_call(partial(mlp_kernel, packed=dp if in_blocks else 0), grid=(...]
    reshape x19 -> x0, local copies, waits for them, and re-layouts: 149 us -> none  [the longest x2 25.7 us: on_device(): win_q = win_q.reshape(head_shape)]
    all_gather x7 -> x0, blocking collectives: 134 us -> none  [the longest x1 43.1 us: fetch_attention(): lax.all_gather(biases, 'fsdp', axis=1, tiled=True)]
    unnamed x15 -> x2, waiting for transfers between devices: 127 us -> 0.03 us
    ppermute x12 -> x25, waiting for transfers between devices: 7.8 us -> 45.9 us  [the longest x19 30.6 us: swap_by(): return lax.ppermute(x, axis, pairs)]
    reduce_sum x17 -> x0, other arithmetic: 27.7 us -> none  [the longest x2 11.2 us: attend_forward(): row_sum = jnp.sum(shifted, axis=-1, keepdims=True)]
  transfers between devices with their start and end apart: 25 -> 27, of which waited for: 12 -> 8; matrix products, arithmetic and copies ran while one was open for 27% -> 6% of each run, Pallas kernels for 0% -> 38%
where the time goes in v1:
time: 280 us; the launch traced here: 279 us
  Pallas kernels  165 us (59%)
  waiting for transfers between devices  46 us (16%)
  starting transfers between devices  32.7 us (12%)
  between operations  14.3 us (5%)
  local copies, waits for them, and re-layouts  13 us (5%)
  other arithmetic  7.95 us (3%)
    pallas_call x1, Pallas kernels, on_device(): pl.pallas_call(partial(mlp_kernel, packed=dp if in_blocks else 0), grid=(...  56.3 us
    pallas_call x2, Pallas kernels, window_forward(): pl.pallas_call(window_forward_kernel, grid=(count,), in_specs=[tiled((gro...  35.5 us
    pallas_call x1, Pallas kernels, on_device(): pl.pallas_call(partial(window_backward_kernel, local_len=local_len), grid...  35 us
    ppermute x19, waiting for transfers between devices, swap_by(): return lax.ppermute(x, axis, pairs)  30.6 us
    ppermute x19, starting transfers between devices, swap_by(): return lax.ppermute(x, axis, pairs)  22.9 us
    pallas_call x3, Pallas kernels, local_back(): pl.pallas_call(local_back_kernel, grid=(count,), in_specs=[tiled((group,...  17.3 us
    ppermute x6, waiting for transfers between devices, matched(): return lax.ppermute(x, axes, pairs)  15.4 us
    unnamed x38, local copies, waits for them, and re-layouts  11.5 us
  transfers between devices with their start and end apart: 27, of which 8 were waited for; matrix products, arithmetic and copies ran while one was open for 6% of the time, Pallas kernels for 38%

profile of v1, /device:TPU:0, one launch (start us, length us, event | category | flops | bytes accessed | tf_op | source)
XLA Modules:
  0.0 279.3 jit_solution(6537979929657682846)
XLA Ops:
  7.2 1.8 pack_weights.1
  9.1 3.1 %collective-permute-start.6 = (bf16[1,288,128]{2,1,0:T(8,128)(2,1)}, bf16[1,288,128]{2,1,0:T(8,128)(2,1)S(1)}, u32[]{:S(2)}, u32[]{:S(2)}) collective-permute-start(bf16[1,288,128]{2,1,0:T(8,128)(2,1)} %bitcast.22), channel_id=1, source_target_pairs={{0,4},{1,5},{2,6},{3,7},{4,0},{5,1},{6,2},{7,3},{8,12},{9,13},{10,... | collective-permute-start | bytes 221192 | tf_op jit(solution)/shard_map/ppermute | solution.py:744
  12.2 2.6 collective-permute-start.7
  14.8 1.7 collective-permute-start
  16.5 1.3 collective-permute-start.1
  17.9 2.3 collective-permute-done.7
  20.2 1.1 collective-permute-done.8
  21.3 0.9 pad_maximum_fusion.refs_7_
  22.3 1.5 collective-permute-start.9
  23.8 1.5 collective-permute-start.10
  25.9 1.6 collective-permute-start.2
  27.6 0.7 collective-permute-start.3
  28.3 12.9 %collective-permute-done.2.refs_3_ = bf16[48,512]{1,0:T(8,128)(2,1)S(1)} collective-permute-done((bf16[48,512]{1,0:T(8,128)(2,1)}, bf16[48,512]{1,0:T(8,128)(2,1)S(1)}, u32[]{:S(2)}, u32[]{:S(2)}) %collective-permute-start.2) | collective-permute-done | bytes 49184 | tf_op jit(solution)/shard_map/ppermute | solution.py:815
  42.2 3.8 %collective-permute-start.4 = (bf16[48,512]{1,0:T(8,128)(2,1)}, bf16[48,512]{1,0:T(8,128)(2,1)S(1)}, u32[]{:S(2)}, u32[]{:S(2)}) collective-permute-start(bf16[48,512]{1,0:T(8,128)(2,1)} %x_ref.1), channel_id=1, source_target_pairs={{0,3},{1,4},{2,5},{3,0},{4,1},{5,2},{6,9},{7,10},{8,11},{9,6},{10,... | collective-permute-start | bytes 147464 | tf_op jit(solution)/shard_map/ppermute | solution.py:815
  46.0 0.8 reshape_select_fusion.kid_ref
  46.8 2.5 collective-permute-done.4.refs_5_
  49.3 0.7 collective-permute-start.5
  50.0 0.6 pad_add_fusion.place_ref
  50.7 0.6 broadcast_in_dim_tile.3.qid_ref
  51.3 2.8 %copy.50.local_ref = bf16[48,49,512]{2,1,0:T(8,128)(2,1)} copy(bf16[48,49,512]{2,0,1:T(8,128)(2,1)S(1)} %copy-done.2) | data formatting | bytes 4816896 | tf_op args[1]
  54.3 0.5 copy-done.16
  54.8 6.2 %region_forward.1 = (f32[48,512]{1,0:T(8,128)}, bf16[336,512]{1,0:T(8,128)(2,1)}, bf16[336,1536]{1,0:T(8,128)(2,1)}, bf16[4,336,256]{2,1,0:T(8,128)(2,1)}, bf16[...) custom-call(s32[2]{0:T(128)} %pad_add_fusion.place_ref, ...), custom_call_target="tpu_custom_call" | custom-call | flops 6600000000 | bytes 6000000 | tf_op jit(solution)/shard_map/region_forward/pallas_call | solution.py:975
  61.0 17.8 %window_forward.2 = (f32[2688,512]{1,0:T(8,128)}, bf16[2688,512]{1,0:T(8,128)(2,1)}, bf16[48,64,1536]{2,1,0:T(8,128)(2,1)}, bf16[48,4,64,256]{3,2,1,0:T(8,128)(2...) custom-call(bf16[48,49,512]{2,1,0:T(8,128)(2,1)} %copy.50.local_ref, f32[48,512]{1,0:T(8,128)} %get-tuple-element.68.row_ref.mid_ref, ...), custom_call_target="tpu_custom_call" | custom-call | flops 19800000512 | bytes 18000000 | tf_op jit(solution)/shard_map/window_forward/pallas_call | solution.py:1021
  78.9 3.8 %collective-permute-start.16 = (bf16[16,256,256]{2,1,0:T(8,128)(2,1)}, bf16[16,256,256]{2,1,0:T(8,128)(2,1)}, u32[]{:S(2)}, u32[]{:S(2)}) collective-permute-start(bf16[16,256,256]{2,1,0:T(8,128)(2,1)} %bitcast.27), channel_id=1, source_target_pairs={{0,16},{16,0},{1,17},{17,1},{2,18},{18,2},{3,19},{19,3},{4,20},{20... | collective-permute-start | bytes 6291464 | tf_op jit(solution)/shard_map/ppermute | solution.py:744
  82.6 2.9 %copy.51.cot_ref = bf16[48,49,512]{2,1,0:T(8,128)(2,1)} copy(bf16[48,49,512]{2,0,1:T(8,128)(2,1)S(1)} %copy-done.3) | data formatting | bytes 4816896 | tf_op args[10]
  85.5 17.6 %window_forward.3 = (f32[2688,512]{1,0:T(8,128)}, bf16[2688,512]{1,0:T(8,128)(2,1)}, bf16[48,64,1536]{2,1,0:T(8,128)(2,1)}, bf16[48,4,64,256]{3,2,1,0:T(8,128)(2...) custom-call(bf16[48,49,512]{2,1,0:T(8,128)(2,1)} %copy.50.local_ref,, ...), custom_call_target="tpu_custom_call", output_to_operand_aliasing={{0}: (5, {}), {1}: (6, {}), {2}: (7, {}), {3}: (8, {}), {4}... | custom-call | flops 19800000512 | bytes 18000000 | tf_op jit(solution)/shard_map/window_forward/pallas_call | solution.py:1021
  103.1 56.3 %mlp.1 = (bf16[48,49,512]{2,1,0:T(8,128)(2,1)}, bf16[48,512]{1,0:T(8,128)(2,1)}, f32[2688,512]{1,0:T(8,128)}, f32[48,512]{1,0:T(8,128)}, bf16[2688,512]{1,0:T(8,...) custom-call(s32[2]{0:T(128)} %pad_add_fusion.place_ref, ...), custom_call_target="tpu_custom_call" | custom-call | flops 54999998464 | bytes 50000000 | tf_op jit(solution)/shard_map/mlp/pallas_call | solution.py:1100
  159.5 4.4 %collective-permute-done.17 = bf16[16,512,128]{2,1,0:T(8,128)(2,1)S(1)} collective-permute-done((bf16[16,512,128]{2,1,0:T(8,128)(2,1)}, bf16[16,512,128]{2,1,0:T(8,128)(2,1)S(1)}, u32[]{:S(2)}, u32[]{:S(2)}) %collective-permute-start.17) | collective-permute-done | bytes 2097184 | tf_op jit(solution)/shard_map/ppermute | solution.py:744
  163.8 3.5 %add_convert_fusion.refs_0_ = bf16[16,512,128]{2,1,0:T(8,128)(2,1)} fusion(bf16[16,512,128]{2,1,0:T(8,128)(2,1)S(1)} %collective-permute-done.17, bf16[16,512,128]{2,1,0:T(8,128)(2,1)} %get-tuple-element.89), kind=kLoop, calls=%fused_computation | loop fusion | flops 4194304 | bytes 6291456 | tf_op jit(solution)/shard_map/convert_element_type | solution.py:1123
  167.3 35.0 %window_backward.1 = (bf16[2688,1536]{1,0:T(8,128)(2,1)}, bf16[48,1536]{1,0:T(8,128)(2,1)}, f32[8,1536]{1,0:T(8,128)}, f32[512,1536]{1,0:T(8,128)}, f32[512,512]{1,0:T(8,128)}) custom-call(bf16[2688,512]{1,0:T(8,128)(2,1)} %get-tuple-element.84.e_ref, bf16[48,64,1536]{2,1,0:T(8,128)(2,1)} %get-tuple-element.85.qkv_ref, ...), custom_call_target="tpu_custom_call" | custom-call | tf_op jit(solution)/shard_map/window_backward/pallas_call | solution.py:1126
  202.4 11.0 %region_tail.1 = (f32[48,512]{1,0:T(8,128)}, bf16[4,4,480,128]{3,2,1,0:T(8,128)(2,1)}, bf16[4,4,480,128]{3,2,1,0:T(8,128)(2,1)}) custom-call(s32[2]{0:T(128)} %pad_add_fusion.place_ref, bf16[48,1536]{1,0:T(8,128)(2,1)} %get-tuple-element.91.mixed_row_ref, f32[48,512]{1,0:T(8,128)} %get-tuple-element.92.dz_row_ref, ...), custom_call_target="tpu_custom_call" | custom-call | tf_op jit(solution)/shard_map/region_tail/pallas_call | solution.py:1186
  213.5 5.9 %local_back.3 = (bf16[48,49,512]{2,1,0:T(8,128)(2,1)}, f32[8,128]{1,0:T(8,128)}) custom-call(bf16[48,49,512]{2,1,0:T(8,128)(2,1)} %copy.50.local_ref, f32[2688,512]{1,0:T(8,128)} %get-tuple-element.104.dz_ref, bf16[2688,1536]{1,0:T(8,128)(2,1)} %get-tuple-element.105.mixed_ref, bf16[512,1536]{1,0:T(8,128)(2,1)} %get-tuple-element.69.wqkv_ref, ...), custom_call_target="tpu_custom_call" | custom-call | flops 6600000000 | bytes 6000000 | tf_op jit(solution)/shard_map/local_back/pallas_call | solution.py:1203
  219.4 1.6 fusion
  221.0 1.3 collective-permute-start.19
  222.3 1.9 collective-permute-start.20
  224.2 1.1 collective-permute-start.21
  225.3 5.7 %local_back.4 = (bf16[48,49,512]{2,1,0:T(8,128)(2,1)}, f32[8,128]{1,0:T(8,128)}) custom-call(bf16[48,49,512]{2,1,0:T(8,128)(2,1)} %copy.50.local_ref, f32[2688,512]{1,0:T(8,128)} %get-tuple-element.104.dz_ref, bf16[2688,1536]{1,0:T(8,128)(2,1)} %get-tuple-element.105.mixed_ref, ...), custom_call_target="tpu_custom_call", output_to_operand_aliasing={{0}: (5, {})} | custom-call | flops 6600000000 | bytes 6000000 | tf_op jit(solution)/shard_map/local_back/pallas_call | solution.py:1203
  231.0 5.8 %local_back.5 = (bf16[48,49,512]{2,1,0:T(8,128)(2,1)}, f32[8,128]{1,0:T(8,128)}) custom-call(bf16[48,49,512]{2,1,0:T(8,128)(2,1)} %copy.50.local_ref, f32[2688,512]{1,0:T(8,128)} %get-tuple-element.104.dz_ref, bf16[2688,1536]{1,0:T(8,128)(2,1)} %get-tuple-element.105.mixed_ref, ...), custom_call_target="tpu_custom_call", output_to_operand_aliasing={{0}: (5, {})} | custom-call | flops 6600000000 | bytes 6000000 | tf_op jit(solution)/shard_map/local_back/pallas_call | solution.py:1203
  236.8 7.5 %collective-permute-done.19 = bf16[4,480,128]{2,1,0:T(8,128)(2,1)S(1)} collective-permute-done((bf16[4,480,128]{2,1,0:T(8,128)(2,1)}, bf16[4,480,128]{2,1,0:T(8,128)(2,1)S(1)}, u32[]{:S(2)}, u32[]{:S(2)}) %collective-permute-start.19) | collective-permute-done | bytes 491552 | tf_op jit(solution)/shard_map/ppermute | solution.py:744
  244.4 11.8 %collective-permute-done.21 = bf16[4,480,128]{2,1,0:T(8,128)(2,1)S(1)} collective-permute-done((bf16[4,480,128]{2,1,0:T(8,128)(2,1)}, bf16[4,480,128]{2,1,0:T(8,128)(2,1)S(1)}, u32[]{:S(2)}, u32[]{:S(2)}) %collective-permute-start.21) | collective-permute-done | bytes 491552 | tf_op jit(solution)/shard_map/ppermute | solution.py:744
  256.4 0.7 slice_bitcast_fusion
  257.1 1.9 collective-permute-start.23
  259.0 2.5 collective-permute-start.24
  261.5 2.3 copy.55
  263.7 2.3 copy.56
  266.0 3.5 %collective-permute-done.23.refs_2_ = bf16[480,128]{1,0:T(8,128)(2,1)S(1)} collective-permute-done((bf16[480,128]{1,0:T(8,128)(2,1)S(1)}, bf16[480,128]{1,0:T(8,128)(2,1)S(1)}, u32[]{:S(2)}, u32[]{:S(2)}) %collective-permute-start.23) | collective-permute-done | bytes 122912 | tf_op jit(solution)/shard_map/ppermute | solution.py:744
  269.5 0.6 copy-done.11
  270.2 2.2 finish.1
  (74 shorter events, 2.7 us)
Async XLA Ops:
  7.2 10.6 %copy-start.7 = (s32[32]{0:T(128)S(1)}, s32[32]{0:T(128)}, u32[]{:S(2)}) copy-start(s32[32]{0:T(128)} %param.19) | copy-start | bytes 388
  7.2 44.2 %copy-start.2 = (bf16[48,49,512]{2,0,1:T(8,128)(2,1)S(1)}, bf16[48,49,512]{2,0,1:T(8,128)(2,1)}, u32[]{:S(2)}) copy-start(bf16[48,49,512]{2,0,1:T(8,128)(2,1)} %param.12) | copy-start | bytes 7225348
  7.2 71.7 %all-gather.3.cloned.1.call-start = ((), (), s32[]{:S(2)}) async-start(), calls=%async_computation.2 | async-start | bytes 2228224 | tf_op jit(solution)/shard_map/all_gather | solution.py:939
  9.1 260.4 %reduce-scatter.2.cloned.1.call-start = ((), (), s32[]{:S(2)}) async-start(), calls=%async_computation.1 | async-start | bytes 2228224 | tf_op jit(solution)/shard_map/reduce_scatter | solution.py:1124
  9.1 8.8 %collective-permute-start.6 = (bf16[1,288,128]{2,1,0:T(8,128)(2,1)}, bf16[1,288,128]{2,1,0:T(8,128)(2,1)S(1)}, u32[]{:S(2)}, u32[]{:S(2)}) collective-permute-start(bf16[1,288,128]{2,1,0:T(8,128)(2,1)} %bitcast.22), channel_id=1, source_target_pairs={{0,4},{1,5},{2,6},{3,7},{4,0},{5,1},{6,2},{7,3},{8,12},{9,13},{10,... | collective-permute-start | bytes 221192 | tf_op jit(solution)/shard_map/ppermute | solution.py:744
  12.2 8.0 %collective-permute-start.7 = (bf16[1,288,128]{2,1,0:T(8,128)(2,1)}, bf16[1,288,128]{2,1,0:T(8,128)(2,1)S(1)}, u32[]{:S(2)}, u32[]{:S(2)}) collective-permute-start(bf16[1,288,128]{2,1,0:T(8,128)(2,1)} %bitcast.23), channel_id=1, source_target_pairs={{0,8},{1,9},{2,10},{3,11},{4,12},{5,13},{6,14},{7,15},{8,0},{9,1},... | collective-permute-start | bytes 221192 | tf_op jit(solution)/shard_map/ppermute | solution.py:744
  14.8 6.5 %collective-permute-start.8 = (bf16[1,288,128]{2,1,0:T(8,128)(2,1)}, bf16[1,288,128]{2,1,0:T(8,128)(2,1)S(1)}, u32[]{:S(2)}, u32[]{:S(2)}) collective-permute-start(bf16[1,288,128]{2,1,0:T(8,128)(2,1)} %bitcast.24), channel_id=1, source_target_pairs={{0,12},{1,13},{2,14},{3,15},{4,8},{5,9},{6,10},{7,11},{8,4},{9,5},... | collective-permute-start | bytes 221192 | tf_op jit(solution)/shard_map/ppermute | solution.py:744
  14.8 11.1 %collective-permute-start = (bf16[48,512]{1,0:T(8,128)(2,1)}, bf16[48,512]{1,0:T(8,128)(2,1)}, u32[]{:S(2)}, u32[]{:S(2)}) collective-permute-start(bf16[48,512]{1,0:T(8,128)(2,1)} %x_ref.1), channel_id=1, source_target_pairs={{0,1},{1,0},{2,3},{3,2},{4,5},{5,4},{6,7},{7,6},{8,9},{9,8},{10,11... | collective-permute-start | bytes 147464 | tf_op jit(solution)/shard_map/ppermute | solution.py:815
  16.5 11.1 %collective-permute-start.1 = (bf16[48,512]{1,0:T(8,128)(2,1)}, bf16[48,512]{1,0:T(8,128)(2,1)}, u32[]{:S(2)}, u32[]{:S(2)}) collective-permute-start(bf16[48,512]{1,0:T(8,128)(2,1)} %x_ref.1), channel_id=1, source_target_pairs={{1,2},{2,1},{3,4},{4,3},{5,6},{6,5},{7,8},{8,7},{9,10},{10,9},{11,... | collective-permute-start | bytes 147464 | tf_op jit(solution)/shard_map/ppermute | solution.py:815
  22.2 32.0 %copy-start.6 = (bf16[4,288,128]{2,1,0:T(8,128)(2,1)}, bf16[4,288,128]{2,1,0:T(8,128)(2,1)S(1)}, u32[]{:S(2)}) copy-start(bf16[4,288,128]{2,1,0:T(8,128)(2,1)S(1)} %pad_maximum_fusion.refs_7_) | copy-start | bytes 884740
  22.3 18.9 %collective-permute-start.9 = (bf16[4,288,128]{2,1,0:T(8,128)(2,1)S(1)}, bf16[4,288,128]{2,1,0:T(8,128)(2,1)S(1)}, u32[]{:S(2)}, u32[]{:S(2)}) collective-permute-start(bf16[4,288,128]{2,1,0:T(8,128)(2,1)S(1)} %pad_maximum_fusion.refs_7_), channel_id=1, source_target_pairs={{0,1},{1,0},{2,3},{3,2},{4,5},{5,4},{6,7},{7,6},{8,9},{9,8},{10,11... | collective-permute-start | bytes 884744 | tf_op jit(solution)/shard_map/ppermute | solution.py:744
  23.8 17.9 %collective-permute-start.10 = (bf16[4,288,128]{2,1,0:T(8,128)(2,1)S(1)}, bf16[4,288,128]{2,1,0:T(8,128)(2,1)S(1)}, u32[]{:S(2)}, u32[]{:S(2)}) collective-permute-start(bf16[4,288,128]{2,1,0:T(8,128)(2,1)S(1)} %pad_maximum_fusion.refs_7_), channel_id=1, source_target_pairs={{0,2},{1,3},{2,0},{3,1},{4,6},{5,7},{6,4},{7,5},{8,10},{9,11},{10,... | collective-permute-start | bytes 884744 | tf_op jit(solution)/shard_map/ppermute | solution.py:744
  25.3 16.5 %collective-permute-start.11 = (bf16[4,288,128]{2,1,0:T(8,128)(2,1)S(1)}, bf16[4,288,128]{2,1,0:T(8,128)(2,1)}, u32[]{:S(2)}, u32[]{:S(2)}) collective-permute-start(bf16[4,288,128]{2,1,0:T(8,128)(2,1)S(1)} %pad_maximum_fusion.refs_7_), channel_id=1, source_target_pairs={{0,3},{1,2},{2,1},{3,0},{4,7},{5,6},{6,5},{7,4},{8,11},{9,10},{10,... | collective-permute-start | bytes 884744 | tf_op jit(solution)/shard_map/ppermute | solution.py:744
  25.9 15.2 %collective-permute-start.2 = (bf16[48,512]{1,0:T(8,128)(2,1)}, bf16[48,512]{1,0:T(8,128)(2,1)S(1)}, u32[]{:S(2)}, u32[]{:S(2)}) collective-permute-start(bf16[48,512]{1,0:T(8,128)(2,1)} %x_ref.1), channel_id=1, source_target_pairs={{0,2},{1,3},{2,0},{3,1},{4,6},{5,7},{6,4},{7,5},{8,10},{9,11},{10,... | collective-permute-start | bytes 147464 | tf_op jit(solution)/shard_map/ppermute | solution.py:815
  27.6 14.6 %collective-permute-start.3 = (bf16[48,512]{1,0:T(8,128)(2,1)}, bf16[48,512]{1,0:T(8,128)(2,1)S(1)}, u32[]{:S(2)}, u32[]{:S(2)}) collective-permute-start(bf16[48,512]{1,0:T(8,128)(2,1)} %x_ref.1), channel_id=1, source_target_pairs={{2,4},{3,5},{4,2},{5,3},{6,8},{7,9},{8,6},{9,7},{10,12},{11,13},{1... | collective-permute-start | bytes 147464 | tf_op jit(solution)/shard_map/ppermute | solution.py:815
  41.2 13.1 %copy-start.13 = (bf16[48,512]{1,0:T(8,128)(2,1)}, bf16[48,512]{1,0:T(8,128)(2,1)S(1)}, u32[]{:S(2)}) copy-start(bf16[48,512]{1,0:T(8,128)(2,1)S(1)} %collective-permute-done.2.refs_3_) | copy-start | bytes 147460
  41.2 13.0 %collective-permute-start.12 = (bf16[4,288,128]{2,1,0:T(8,128)(2,1)S(1)}, bf16[4,288,128]{2,1,0:T(8,128)(2,1)}, u32[]{:S(2)}, u32[]{:S(2)}) collective-permute-start(bf16[4,288,128]{2,1,0:T(8,128)(2,1)S(1)} %pad_maximum_fusion.refs_7_), channel_id=1, source_target_pairs={{0,16},{16,0},{1,17},{17,1},{2,18},{18,2},{3,19},{19,3},{4,20},{20... | collective-permute-start | bytes 884744 | tf_op jit(solution)/shard_map/ppermute | solution.py:744
  41.2 13.1 %copy-start.8 = (bf16[4,288,128]{2,1,0:T(8,128)(2,1)}, bf16[4,288,128]{2,1,0:T(8,128)(2,1)S(1)}, u32[]{:S(2)}) copy-start(bf16[4,288,128]{2,1,0:T(8,128)(2,1)S(1)} %collective-permute-done.9.refs_8_) | copy-start | bytes 884740
  41.2 13.0 %collective-permute-start.13 = (bf16[4,288,128]{2,1,0:T(8,128)(2,1)S(1)}, bf16[4,288,128]{2,1,0:T(8,128)(2,1)}, u32[]{:S(2)}, u32[]{:S(2)}) collective-permute-start(bf16[4,288,128]{2,1,0:T(8,128)(2,1)S(1)} %collective-permute-done.9.refs_8_), channel_id=1, source_target_pairs={{0,16},{16,0},{1,17},{17,1},{2,18},{18,2},{3,19},{19,3},{4,20},{20... | collective-permute-start | bytes 884744 | tf_op jit(solution)/shard_map/ppermute | solution.py:744
  41.7 12.6 %copy-start.9 = (bf16[4,288,128]{2,1,0:T(8,128)(2,1)}, bf16[4,288,128]{2,1,0:T(8,128)(2,1)S(1)}, u32[]{:S(2)}) copy-start(bf16[4,288,128]{2,1,0:T(8,128)(2,1)S(1)} %collective-permute-done.10.refs_9_) | copy-start | bytes 884740
  41.7 12.5 %collective-permute-start.14 = (bf16[4,288,128]{2,1,0:T(8,128)(2,1)S(1)}, bf16[4,288,128]{2,1,0:T(8,128)(2,1)}, u32[]{:S(2)}, u32[]{:S(2)}) collective-permute-start(bf16[4,288,128]{2,1,0:T(8,128)(2,1)S(1)} %collective-permute-done.10.refs_9_), channel_id=1, source_target_pairs={{0,16},{16,0},{1,17},{17,1},{2,18},{18,2},{3,19},{19,3},{4,20},{20... | collective-permute-start | bytes 884744 | tf_op jit(solution)/shard_map/ppermute | solution.py:744
  41.8 12.5 %collective-permute-start.15 = (bf16[4,288,128]{2,1,0:T(8,128)(2,1)}, bf16[4,288,128]{2,1,0:T(8,128)(2,1)}, u32[]{:S(2)}, u32[]{:S(2)}) collective-permute-start(bf16[4,288,128]{2,1,0:T(8,128)(2,1)} %collective-permute-done.11.refs_10_), channel_id=1, source_target_pairs={{0,16},{16,0},{1,17},{17,1},{2,18},{18,2},{3,19},{19,3},{4,20},{20... | collective-permute-start | bytes 884744 | tf_op jit(solution)/shard_map/ppermute | solution.py:744
  42.2 12.1 %copy-start.14 = (bf16[48,512]{1,0:T(8,128)(2,1)}, bf16[48,512]{1,0:T(8,128)(2,1)S(1)}, u32[]{:S(2)}) copy-start(bf16[48,512]{1,0:T(8,128)(2,1)S(1)} %collective-permute-done.3.refs_4_) | copy-start | bytes 147460
  42.2 7.1 %collective-permute-start.4 = (bf16[48,512]{1,0:T(8,128)(2,1)}, bf16[48,512]{1,0:T(8,128)(2,1)S(1)}, u32[]{:S(2)}, u32[]{:S(2)}) collective-permute-start(bf16[48,512]{1,0:T(8,128)(2,1)} %x_ref.1), channel_id=1, source_target_pairs={{0,3},{1,4},{2,5},{3,0},{4,1},{5,2},{6,9},{7,10},{8,11},{9,6},{10,... | collective-permute-start | bytes 147464 | tf_op jit(solution)/shard_map/ppermute | solution.py:815
  49.3 5.0 %copy-start.15 = (bf16[48,512]{1,0:T(8,128)(2,1)}, bf16[48,512]{1,0:T(8,128)(2,1)S(1)}, u32[]{:S(2)}) copy-start(bf16[48,512]{1,0:T(8,128)(2,1)S(1)} %collective-permute-done.4.refs_5_) | copy-start | bytes 147460
  49.3 4.9 %collective-permute-start.5 = (bf16[48,512]{1,0:T(8,128)(2,1)}, bf16[48,512]{1,0:T(8,128)(2,1)S(1)}, u32[]{:S(2)}, u32[]{:S(2)}) collective-permute-start(bf16[48,512]{1,0:T(8,128)(2,1)} %x_ref.1), channel_id=1, source_target_pairs={{3,6},{4,7},{5,8},{6,3},{7,4},{8,5},{9,12},{10,13},{11,14},{12,9},... | collective-permute-start | bytes 147464 | tf_op jit(solution)/shard_map/ppermute | solution.py:815
  54.2 0.6 copy-start.16
  61.0 21.6 %copy-start.3 = (bf16[48,49,512]{2,0,1:T(8,128)(2,1)S(1)}, bf16[48,49,512]{2,0,1:T(8,128)(2,1)}, u32[]{:S(2)}) copy-start(bf16[48,49,512]{2,0,1:T(8,128)(2,1)} %param.21) | copy-start | bytes 7225348
  78.9 24.2 %collective-permute-start.16 = (bf16[16,256,256]{2,1,0:T(8,128)(2,1)}, bf16[16,256,256]{2,1,0:T(8,128)(2,1)}, u32[]{:S(2)}, u32[]{:S(2)}) collective-permute-start(bf16[16,256,256]{2,1,0:T(8,128)(2,1)} %bitcast.27), channel_id=1, source_target_pairs={{0,16},{16,0},{1,17},{17,1},{2,18},{18,2},{3,19},{19,3},{4,20},{20... | collective-permute-start | bytes 6291464 | tf_op jit(solution)/shard_map/ppermute | solution.py:744
  159.4 4.4 %collective-permute-start.17 = (bf16[16,512,128]{2,1,0:T(8,128)(2,1)}, bf16[16,512,128]{2,1,0:T(8,128)(2,1)S(1)}, u32[]{:S(2)}, u32[]{:S(2)}) collective-permute-start(bf16[16,512,128]{2,1,0:T(8,128)(2,1)} %get-tuple-element.90), channel_id=1, source_target_pairs={{0,16},{16,0},{1,17},{17,1},{2,18},{18,2},{3,19},{19,3},{4,20},{20... | collective-permute-start | bytes 6291464 | tf_op jit(solution)/shard_map/ppermute | solution.py:744
  213.3 6.0 %collective-permute-start.18 = (bf16[4,4,480,128]{3,2,1,0:T(8,128)(2,1)}, bf16[4,4,480,128]{3,2,1,0:T(8,128)(2,1)S(1)}, u32[]{:S(2)}, u32[]{:S(2)}) collective-permute-start(bf16[4,4,480,128]{3,2,1,0:T(8,128)(2,1)} %get-tuple-element.103), channel_id=1, source_target_pairs={{0,16},{16,0},{1,17},{17,1},{2,18},{18,2},{3,19},{19,3},{4,20},{20... | collective-permute-start | bytes 5898248 | tf_op jit(solution)/shard_map/ppermute | solution.py:744
  213.5 5.9 %copy-start.5 = (bf16[4,4,480,128]{3,2,1,0:T(8,128)(2,1)S(1)}, bf16[4,4,480,128]{3,2,1,0:T(8,128)(2,1)}, u32[]{:S(2)}) copy-start(bf16[4,4,480,128]{3,2,1,0:T(8,128)(2,1)} %get-tuple-element.102.refs_0_) | copy-start | bytes 5898244
  221.0 23.4 %collective-permute-start.19 = (bf16[4,480,128]{2,1,0:T(8,128)(2,1)}, bf16[4,480,128]{2,1,0:T(8,128)(2,1)S(1)}, u32[]{:S(2)}, u32[]{:S(2)}) collective-permute-start(bf16[4,480,128]{2,1,0:T(8,128)(2,1)} %get-tuple-element.157), channel_id=1, source_target_pairs={{0,1},{1,0},{2,3},{3,2},{4,5},{5,4},{6,7},{7,6},{8,9},{9,8},{10,11... | collective-permute-start | bytes 1474568 | tf_op jit(solution)/shard_map/ppermute | solution.py:744
  222.3 22.0 %collective-permute-start.20 = (bf16[4,480,128]{2,1,0:T(8,128)(2,1)}, bf16[4,480,128]{2,1,0:T(8,128)(2,1)S(1)}, u32[]{:S(2)}, u32[]{:S(2)}) collective-permute-start(bf16[4,480,128]{2,1,0:T(8,128)(2,1)} %get-tuple-element.156), channel_id=1, source_target_pairs={{0,2},{1,3},{2,0},{3,1},{4,6},{5,7},{6,4},{7,5},{8,10},{9,11},{10,... | collective-permute-start | bytes 1474568 | tf_op jit(solution)/shard_map/ppermute | solution.py:744
  224.2 31.9 %collective-permute-start.21 = (bf16[4,480,128]{2,1,0:T(8,128)(2,1)}, bf16[4,480,128]{2,1,0:T(8,128)(2,1)S(1)}, u32[]{:S(2)}, u32[]{:S(2)}) collective-permute-start(bf16[4,480,128]{2,1,0:T(8,128)(2,1)} %get-tuple-element.155), channel_id=1, source_target_pairs={{0,3},{1,2},{2,1},{3,0},{4,7},{5,6},{6,5},{7,4},{8,11},{9,10},{10,... | collective-permute-start | bytes 1474568 | tf_op jit(solution)/shard_map/ppermute | solution.py:744
  231.0 25.1 %copy-start.4 = (bf16[4,480,128]{2,1,0:T(8,128)(2,1)S(1)}, bf16[4,480,128]{2,1,0:T(8,128)(2,1)}, u32[]{:S(2)}) copy-start(bf16[4,480,128]{2,1,0:T(8,128)(2,1)} %get-tuple-element.154.refs_2_) | copy-start | bytes 1474564
  236.8 24.6 %copy-start = (bf16[48,49,512]{2,1,0:T(8,128)(2,1)S(1)}, bf16[48,49,512]{2,1,0:T(8,128)(2,1)}, u32[]{:S(2)}) copy-start(bf16[48,49,512]{2,1,0:T(8,128)(2,1)} %get-tuple-element.145) | copy-start | bytes 7225348
  257.1 6.7 %copy-start.1 = (bf16[48,49,512]{2,1,0:T(8,128)(2,1)S(1)}, bf16[48,49,512]{2,1,0:T(8,128)(2,1)}, u32[]{:S(2)}) copy-start(bf16[48,49,512]{2,1,0:T(8,128)(2,1)} %get-tuple-element.147) | copy-start | bytes 7225348
  257.1 8.9 %collective-permute-start.22 = (bf16[480,128]{1,0:T(8,128)(2,1)S(1)}, bf16[480,128]{1,0:T(8,128)(2,1)S(1)}, u32[]{:S(2)}, u32[]{:S(2)}) collective-permute-start(bf16[480,128]{1,0:T(8,128)(2,1)S(1)} %get-tuple-element.160), channel_id=1, source_target_pairs={{0,4},{1,5},{2,6},{3,7},{4,0},{5,1},{6,2},{7,3},{8,12},{9,13},{10,... | collective-permute-start | bytes 368648 | tf_op jit(solution)/shard_map/ppermute | solution.py:744
  257.1 12.4 %collective-permute-start.23 = (bf16[480,128]{1,0:T(8,128)(2,1)S(1)}, bf16[480,128]{1,0:T(8,128)(2,1)S(1)}, u32[]{:S(2)}, u32[]{:S(2)}) collective-permute-start(bf16[480,128]{1,0:T(8,128)(2,1)S(1)} %get-tuple-element.159), channel_id=1, source_target_pairs={{0,8},{1,9},{2,10},{3,11},{4,12},{5,13},{6,14},{7,15},{8,0},{9,1},... | collective-permute-start | bytes 368648 | tf_op jit(solution)/shard_map/ppermute | solution.py:744
  259.0 10.5 %collective-permute-start.24 = (bf16[480,128]{1,0:T(8,128)(2,1)S(1)}, bf16[480,128]{1,0:T(8,128)(2,1)S(1)}, u32[]{:S(2)}, u32[]{:S(2)}) collective-permute-start(bf16[480,128]{1,0:T(8,128)(2,1)S(1)} %get-tuple-element.158), channel_id=1, source_target_pairs={{0,12},{1,13},{2,14},{3,15},{4,8},{5,9},{6,10},{7,11},{8,4},{9,5},... | collective-permute-start | bytes 368648 | tf_op jit(solution)/shard_map/ppermute | solution.py:744
  266.0 3.5 %copy-start.10 = (bf16[480,128]{1,0:T(8,128)(2,1)}, bf16[480,128]{1,0:T(8,128)(2,1)S(1)}, u32[]{:S(2)}) copy-start(bf16[480,128]{1,0:T(8,128)(2,1)S(1)} %collective-permute-done.22.refs_1_) | copy-start | bytes 368644
  269.5 0.7 copy-start.11
  269.5 0.7 copy-start.12
Sparse Core Ops, SparseCore 0:
  11.4 64.2 all-gather.2
  167.4 82.8 reduce-scatter.1
